TPU v7x, 32 devices: a whole 2x2x4 slice. The times are simulated.
32 devices in a mesh: row: 2 (over x), col: 16 (over z, y, core).
Axes of the slice: x: 2, y: 2, z: 4, core: 2. Of those that a mesh axis runs over, the one named last changes fastest.
Arguments:
- region_factors: bfloat16 [32768, 512], P(('row', 'col')), may hold values from -1.25 to 1.25
- item_factors: bfloat16 [16, 128, 512], P('col', 'row'), may hold values from -1.25 to 1.25
- slab_blocks: bfloat16 [32, 16, 6, 128, 128], P(('row', 'col')), may hold values from -6 to 6
- block_rows: int32 [32, 16, 6], P(('row', 'col')), may hold values from 0 to 7, as said below
- counts: int32 [32, 16], P(('row', 'col')), may hold values from 1 to 6, as said below
Outputs:
- new_regions: float32 [32768, 512], P(('row', 'col'))
- new_items: float32 [16, 128, 512], P('col', 'row')
Inputs may be any that keep to these rules, and one draw needn't show every extreme that they name: `counts`: every entry is at least 1; some device-block has exactly 6 present blocks in some block column. `block_rows`: for each device-block and block column, the first counts[d, p] entries are distinct; entries at slots s >= counts[d, p] (and their slab blocks) are not used.
All inputs are finite; a program needn't handle non-finite values.
Results may differ from a plain program's by a relative error of at most 0.0023.
Values may be sent and summed in bfloat16 or wider, within the bound.
A program may use at most 128 MiB of HBM per device.

v0:
```python
import jax
import jax.numpy as jnp
from jax import lax
from jax.sharding import PartitionSpec as P

region_rate = 0.05
item_rate = 0.01
decay_rate = 0.1


def passed_along(value, axis, steps):
    count = lax.axis_size(axis)
    pairs = [(source, (source + steps) % count) for source in range(count)]
    return lax.ppermute(value, axis, pairs)


def pass_panel(panel_now):
    return passed_along(panel_now, "col", 1)


def on_device(region_factors, item_factors, slab_blocks, block_rows, counts):
    cycle_size = lax.axis_size("col")
    position = lax.axis_index("col")
    block_size = slab_blocks.shape[-1]
    factor_width = region_factors.shape[-1]
    slot_total = slab_blocks.shape[2]
    row_blocks = region_factors.shape[0] // block_size
    region_blocks = region_factors.reshape(row_blocks, block_size, factor_width)
    tiles_all = slab_blocks[0]
    row_lists = block_rows[0]
    live_counts = counts[0]
    slot_ids = jnp.arange(slot_total, dtype=jnp.int32)
    panel_start = lax.all_gather(item_factors, "row", axis=1, tiled=True)[0]
    region_zero = jnp.zeros((row_blocks, block_size, factor_width), jnp.float32)
    item_zero = jnp.zeros((block_size, factor_width), jnp.float32)

    def padded_work(column, panel_now, region_totals):
        rows_now = lax.dynamic_index_in_dim(row_lists, column, 0, keepdims=False)
        tiles_now = lax.dynamic_index_in_dim(tiles_all, column, 0, keepdims=False)
        count_now = lax.dynamic_index_in_dim(live_counts, column, 0, keepdims=False)
        chosen = jnp.take(region_blocks, rows_now, axis=0)
        predicted = jnp.einsum("sik,jk->sij", chosen, panel_now, preferred_element_type=jnp.float32)
        present = slot_ids < count_now
        residual = jnp.where(present[:, None, None], predicted - tiles_now.astype(jnp.float32), 0.0)
        residual = residual.astype(jnp.bfloat16)
        update = jnp.einsum("sij,jk->sik", residual, panel_now, preferred_element_type=jnp.float32)
        region_totals = region_totals.at[rows_now].add(update)
        item_part = jnp.einsum("sij,sik->jk", residual, chosen, preferred_element_type=jnp.float32)
        return (region_totals, item_part)

    def block_work(column, panel_now, region_totals):
        return padded_work(column, panel_now, region_totals)

    last_column = (position + 1) % cycle_size

    def cycle_travel(passed, carried):
        panel_now, grad_now, region_totals = carried
        column = (position - passed) % cycle_size
        region_totals, item_part = block_work(column, panel_now, region_totals)
        grad_now = grad_now + item_part
        panel_now = pass_panel(panel_now)
        grad_now = passed_along(grad_now, "col", 1)
        return (panel_now, grad_now, region_totals)

    panel_now, grad_now, region_totals = lax.fori_loop(
        0, cycle_size - 1, cycle_travel, (panel_start, item_zero, region_zero)
    )
    region_totals, item_part = block_work(last_column, panel_now, region_totals)
    grad_home = passed_along(grad_now + item_part, "col", 1)
    own_piece = lax.psum_scatter(grad_home, "row", scatter_dimension=0, tiled=True)
    regions_wide = region_factors.astype(jnp.float32)
    region_grad = region_totals.reshape(row_blocks * block_size, factor_width)
    new_regions = regions_wide - region_rate * (region_grad + decay_rate * regions_wide)
    own_rows = item_factors[0].astype(jnp.float32)
    new_items = (own_rows - item_rate * (own_piece + decay_rate * own_rows))[None]
    return (new_regions, new_items)


def solution(mesh):
    return jax.shard_map(
        on_device,
        mesh=mesh,
        in_specs=(
            P(("row", "col"), None),
            P("col", "row", None),
            P(("row", "col"), None, None, None, None),
            P(("row", "col"), None, None),
            P(("row", "col"), None),
        ),
        out_specs=(P(("row", "col"), None), P("col", "row", None)),
        check_vma=False,
    )
```

profile of v0, /device:TPU:0, one launch (start us, length us, event | category | flops | bytes accessed | tf_op | source)
XLA Modules:
  0.0 247.2 jit_solution(9340925826387233154)
XLA Ops:
  11.0 6.1 %all_gather.3 = bf16[1,128,512]{2,1,0:T(8,128)(2,1)S(1)} all-gather(bf16[1,64,512]{2,1,0:T(8,128)(2,1)} %param.10), channel_id=1, replica_groups=mesh['row'=2,'col'=16] {'row'}, dimensions={1}, use_global_device_ids=true | all-gather | bytes 196608 | tf_op jit(solution)/shard_map/all_gather | solution.py:33
  17.1 2.7 %gather_fusion.1 = bf16[6,128,512]{2,1,0:T(8,128)(2,1)} fusion(bf16[8,128,512]{2,1,0:T(8,128)(2,1)} %bitcast.71, s32[1024]{0:T(1024)S(1)} %pad_clamp_fusion.1), kind=kCustom, calls=%fused_computation.1.clone | custom fusion | bytes 1572888 | tf_op jit(solution)/shard_map/jit(_take)/gather | solution.py:41
  19.8 1.6 broadcast_in_dim.68
  21.4 196.4 %while.20 = (s32[]{:T(128)}, bf16[128,512]{1,0:T(8,128)(2,1)S(1)}, f32[128,512]{1,0:T(8,128)S(1)}, f32[8,128,512]{2,1,0:T(8,128)}, s32[]{:T(128)}, /*index=5*/s3...) while((s32[]{:T(128)}, bf16[128,512]{1,0:T(8,128)(2,1)S(1)}, ...), condition=%wide.region_2.4_spmd.clone, body=%wide.region_0.3_spmd.clone.sunk | while | flops 303629376 | bytes 12849738 | solution.py:65
  23.4 1.3 fusion.41
  25.8 2.1 collective-permute-start.1
  28.3 3.9 %scatter_fusion = f32[8,128,512]{2,1,0:T(8,128)} fusion(f32[8,128,512]{2,1,0:T(8,128)} %get-tuple-element.386, s32[6]{0:T(128)S(1)} %fusion.43, f32[6,128,512]{2,1,0:T(8,128)S(1)} %fusion.44), kind=kCustom, calls=%fused_computation.2.clone.clone.1 | custom fusion | flops 393216 | bytes 4718616 | tf_op jit(solution)/shard_map/while/body/eval_jaxpr/scatter-add | solution.py:47
  32.2 2.4 collective-permute-done.1
  36.5 1.3 fusion.41
  39.3 3.9 %scatter_fusion = f32[8,128,512]{2,1,0:T(8,128)} fusion(f32[8,128,512]{2,1,0:T(8,128)} %get-tuple-element.386, s32[6]{0:T(128)S(1)} %fusion.43, f32[6,128,512]{2,1,0:T(8,128)S(1)} %fusion.44), kind=kCustom, calls=%fused_computation.2.clone.clone.1 | custom fusion | flops 393216 | bytes 4718616 | tf_op jit(solution)/shard_map/while/body/eval_jaxpr/scatter-add | solution.py:47
  43.2 4.4 %collective-permute-done.1 = f32[128,512]{1,0:T(8,128)S(1)} collective-permute-done((f32[128,512]{1,0:T(8,128)}, f32[128,512]{1,0:T(8,128)S(1)}, u32[]{:S(2)}, u32[]{:S(2)}) %collective-permute-start.1) | collective-permute-done | bytes 262176 | tf_op jit(solution)/shard_map/while/body/eval_jaxpr/ppermute | solution.py:14
  52.4 3.9 %scatter_fusion = f32[8,128,512]{2,1,0:T(8,128)} fusion(f32[8,128,512]{2,1,0:T(8,128)} %get-tuple-element.386, s32[6]{0:T(128)S(1)} %fusion.43, f32[6,128,512]{2,1,0:T(8,128)S(1)} %fusion.44), kind=kCustom, calls=%fused_computation.2.clone.clone.1 | custom fusion | flops 393216 | bytes 4718616 | tf_op jit(solution)/shard_map/while/body/eval_jaxpr/scatter-add | solution.py:47
  56.3 4.4 %collective-permute-done.1 = f32[128,512]{1,0:T(8,128)S(1)} collective-permute-done((f32[128,512]{1,0:T(8,128)}, f32[128,512]{1,0:T(8,128)S(1)}, u32[]{:S(2)}, u32[]{:S(2)}) %collective-permute-start.1) | collective-permute-done | bytes 262176 | tf_op jit(solution)/shard_map/while/body/eval_jaxpr/ppermute | solution.py:14
  62.7 1.3 fusion.41
  65.5 3.9 %scatter_fusion = f32[8,128,512]{2,1,0:T(8,128)} fusion(f32[8,128,512]{2,1,0:T(8,128)} %get-tuple-element.386, s32[6]{0:T(128)S(1)} %fusion.43, f32[6,128,512]{2,1,0:T(8,128)S(1)} %fusion.44), kind=kCustom, calls=%fused_computation.2.clone.clone.1 | custom fusion | flops 393216 | bytes 4718616 | tf_op jit(solution)/shard_map/while/body/eval_jaxpr/scatter-add | solution.py:47
  69.4 4.4 %collective-permute-done.1 = f32[128,512]{1,0:T(8,128)S(1)} collective-permute-done((f32[128,512]{1,0:T(8,128)}, f32[128,512]{1,0:T(8,128)S(1)}, u32[]{:S(2)}, u32[]{:S(2)}) %collective-permute-start.1) | collective-permute-done | bytes 262176 | tf_op jit(solution)/shard_map/while/body/eval_jaxpr/ppermute | solution.py:14
  75.8 1.3 fusion.41
  78.6 3.9 %scatter_fusion = f32[8,128,512]{2,1,0:T(8,128)} fusion(f32[8,128,512]{2,1,0:T(8,128)} %get-tuple-element.386, s32[6]{0:T(128)S(1)} %fusion.43, f32[6,128,512]{2,1,0:T(8,128)S(1)} %fusion.44), kind=kCustom, calls=%fused_computation.2.clone.clone.1 | custom fusion | flops 393216 | bytes 4718616 | tf_op jit(solution)/shard_map/while/body/eval_jaxpr/scatter-add | solution.py:47
  82.5 4.4 %collective-permute-done.1 = f32[128,512]{1,0:T(8,128)S(1)} collective-permute-done((f32[128,512]{1,0:T(8,128)}, f32[128,512]{1,0:T(8,128)S(1)}, u32[]{:S(2)}, u32[]{:S(2)}) %collective-permute-start.1) | collective-permute-done | bytes 262176 | tf_op jit(solution)/shard_map/while/body/eval_jaxpr/ppermute | solution.py:14
  88.9 1.3 fusion.41
  91.7 3.9 %scatter_fusion = f32[8,128,512]{2,1,0:T(8,128)} fusion(f32[8,128,512]{2,1,0:T(8,128)} %get-tuple-element.386, s32[6]{0:T(128)S(1)} %fusion.43, f32[6,128,512]{2,1,0:T(8,128)S(1)} %fusion.44), kind=kCustom, calls=%fused_computation.2.clone.clone.1 | custom fusion | flops 393216 | bytes 4718616 | tf_op jit(solution)/shard_map/while/body/eval_jaxpr/scatter-add | solution.py:47
  95.6 4.4 %collective-permute-done.1 = f32[128,512]{1,0:T(8,128)S(1)} collective-permute-done((f32[128,512]{1,0:T(8,128)}, f32[128,512]{1,0:T(8,128)S(1)}, u32[]{:S(2)}, u32[]{:S(2)}) %collective-permute-start.1) | collective-permute-done | bytes 262176 | tf_op jit(solution)/shard_map/while/body/eval_jaxpr/ppermute | solution.py:14
  102.0 1.3 fusion.41
  104.8 3.9 %scatter_fusion = f32[8,128,512]{2,1,0:T(8,128)} fusion(f32[8,128,512]{2,1,0:T(8,128)} %get-tuple-element.386, s32[6]{0:T(128)S(1)} %fusion.43, f32[6,128,512]{2,1,0:T(8,128)S(1)} %fusion.44), kind=kCustom, calls=%fused_computation.2.clone.clone.1 | custom fusion | flops 393216 | bytes 4718616 | tf_op jit(solution)/shard_map/while/body/eval_jaxpr/scatter-add | solution.py:47
  108.7 4.4 %collective-permute-done.1 = f32[128,512]{1,0:T(8,128)S(1)} collective-permute-done((f32[128,512]{1,0:T(8,128)}, f32[128,512]{1,0:T(8,128)S(1)}, u32[]{:S(2)}, u32[]{:S(2)}) %collective-permute-start.1) | collective-permute-done | bytes 262176 | tf_op jit(solution)/shard_map/while/body/eval_jaxpr/ppermute | solution.py:14
  117.9 3.9 %scatter_fusion = f32[8,128,512]{2,1,0:T(8,128)} fusion(f32[8,128,512]{2,1,0:T(8,128)} %get-tuple-element.386, s32[6]{0:T(128)S(1)} %fusion.43, f32[6,128,512]{2,1,0:T(8,128)S(1)} %fusion.44), kind=kCustom, calls=%fused_computation.2.clone.clone.1 | custom fusion | flops 393216 | bytes 4718616 | tf_op jit(solution)/shard_map/while/body/eval_jaxpr/scatter-add | solution.py:47
  121.8 4.4 %collective-permute-done.1 = f32[128,512]{1,0:T(8,128)S(1)} collective-permute-done((f32[128,512]{1,0:T(8,128)}, f32[128,512]{1,0:T(8,128)S(1)}, u32[]{:S(2)}, u32[]{:S(2)}) %collective-permute-start.1) | collective-permute-done | bytes 262176 | tf_op jit(solution)/shard_map/while/body/eval_jaxpr/ppermute | solution.py:14
  130.9 3.9 %scatter_fusion = f32[8,128,512]{2,1,0:T(8,128)} fusion(f32[8,128,512]{2,1,0:T(8,128)} %get-tuple-element.386, s32[6]{0:T(128)S(1)} %fusion.43, f32[6,128,512]{2,1,0:T(8,128)S(1)} %fusion.44), kind=kCustom, calls=%fused_computation.2.clone.clone.1 | custom fusion | flops 393216 | bytes 4718616 | tf_op jit(solution)/shard_map/while/body/eval_jaxpr/scatter-add | solution.py:47
  134.8 4.4 %collective-permute-done.1 = f32[128,512]{1,0:T(8,128)S(1)} collective-permute-done((f32[128,512]{1,0:T(8,128)}, f32[128,512]{1,0:T(8,128)S(1)}, u32[]{:S(2)}, u32[]{:S(2)}) %collective-permute-start.1) | collective-permute-done | bytes 262176 | tf_op jit(solution)/shard_map/while/body/eval_jaxpr/ppermute | solution.py:14
  144.0 3.9 %scatter_fusion = f32[8,128,512]{2,1,0:T(8,128)} fusion(f32[8,128,512]{2,1,0:T(8,128)} %get-tuple-element.386, s32[6]{0:T(128)S(1)} %fusion.43, f32[6,128,512]{2,1,0:T(8,128)S(1)} %fusion.44), kind=kCustom, calls=%fused_computation.2.clone.clone.1 | custom fusion | flops 393216 | bytes 4718616 | tf_op jit(solution)/shard_map/while/body/eval_jaxpr/scatter-add | solution.py:47
  147.9 4.4 %collective-permute-done.1 = f32[128,512]{1,0:T(8,128)S(1)} collective-permute-done((f32[128,512]{1,0:T(8,128)}, f32[128,512]{1,0:T(8,128)S(1)}, u32[]{:S(2)}, u32[]{:S(2)}) %collective-permute-start.1) | collective-permute-done | bytes 262176 | tf_op jit(solution)/shard_map/while/body/eval_jaxpr/ppermute | solution.py:14
  157.1 3.9 %scatter_fusion = f32[8,128,512]{2,1,0:T(8,128)} fusion(f32[8,128,512]{2,1,0:T(8,128)} %get-tuple-element.386, s32[6]{0:T(128)S(1)} %fusion.43, f32[6,128,512]{2,1,0:T(8,128)S(1)} %fusion.44), kind=kCustom, calls=%fused_computation.2.clone.clone.1 | custom fusion | flops 393216 | bytes 4718616 | tf_op jit(solution)/shard_map/while/body/eval_jaxpr/scatter-add | solution.py:47
  161.0 4.4 %collective-permute-done.1 = f32[128,512]{1,0:T(8,128)S(1)} collective-permute-done((f32[128,512]{1,0:T(8,128)}, f32[128,512]{1,0:T(8,128)S(1)}, u32[]{:S(2)}, u32[]{:S(2)}) %collective-permute-start.1) | collective-permute-done | bytes 262176 | tf_op jit(solution)/shard_map/while/body/eval_jaxpr/ppermute | solution.py:14
  170.2 3.9 %scatter_fusion = f32[8,128,512]{2,1,0:T(8,128)} fusion(f32[8,128,512]{2,1,0:T(8,128)} %get-tuple-element.386, s32[6]{0:T(128)S(1)} %fusion.43, f32[6,128,512]{2,1,0:T(8,128)S(1)} %fusion.44), kind=kCustom, calls=%fused_computation.2.clone.clone.1 | custom fusion | flops 393216 | bytes 4718616 | tf_op jit(solution)/shard_map/while/body/eval_jaxpr/scatter-add | solution.py:47
  174.2 4.4 %collective-permute-done.1 = f32[128,512]{1,0:T(8,128)S(1)} collective-permute-done((f32[128,512]{1,0:T(8,128)}, f32[128,512]{1,0:T(8,128)S(1)}, u32[]{:S(2)}, u32[]{:S(2)}) %collective-permute-start.1) | collective-permute-done | bytes 262176 | tf_op jit(solution)/shard_map/while/body/eval_jaxpr/ppermute | solution.py:14
  183.3 3.9 %scatter_fusion = f32[8,128,512]{2,1,0:T(8,128)} fusion(f32[8,128,512]{2,1,0:T(8,128)} %get-tuple-element.386, s32[6]{0:T(128)S(1)} %fusion.43, f32[6,128,512]{2,1,0:T(8,128)S(1)} %fusion.44), kind=kCustom, calls=%fused_computation.2.clone.clone.1 | custom fusion | flops 393216 | bytes 4718616 | tf_op jit(solution)/shard_map/while/body/eval_jaxpr/scatter-add | solution.py:47
  187.2 4.4 %collective-permute-done.1 = f32[128,512]{1,0:T(8,128)S(1)} collective-permute-done((f32[128,512]{1,0:T(8,128)}, f32[128,512]{1,0:T(8,128)S(1)}, u32[]{:S(2)}, u32[]{:S(2)}) %collective-permute-start.1) | collective-permute-done | bytes 262176 | tf_op jit(solution)/shard_map/while/body/eval_jaxpr/ppermute | solution.py:14
  196.4 3.9 %scatter_fusion = f32[8,128,512]{2,1,0:T(8,128)} fusion(f32[8,128,512]{2,1,0:T(8,128)} %get-tuple-element.386, s32[6]{0:T(128)S(1)} %fusion.43, f32[6,128,512]{2,1,0:T(8,128)S(1)} %fusion.44), kind=kCustom, calls=%fused_computation.2.clone.clone.1 | custom fusion | flops 393216 | bytes 4718616 | tf_op jit(solution)/shard_map/while/body/eval_jaxpr/scatter-add | solution.py:47
  200.3 4.4 %collective-permute-done.1 = f32[128,512]{1,0:T(8,128)S(1)} collective-permute-done((f32[128,512]{1,0:T(8,128)}, f32[128,512]{1,0:T(8,128)S(1)}, u32[]{:S(2)}, u32[]{:S(2)}) %collective-permute-start.1) | collective-permute-done | bytes 262176 | tf_op jit(solution)/shard_map/while/body/eval_jaxpr/ppermute | solution.py:14
  209.5 3.9 %scatter_fusion = f32[8,128,512]{2,1,0:T(8,128)} fusion(f32[8,128,512]{2,1,0:T(8,128)} %get-tuple-element.386, s32[6]{0:T(128)S(1)} %fusion.43, f32[6,128,512]{2,1,0:T(8,128)S(1)} %fusion.44), kind=kCustom, calls=%fused_computation.2.clone.clone.1 | custom fusion | flops 393216 | bytes 4718616 | tf_op jit(solution)/shard_map/while/body/eval_jaxpr/scatter-add | solution.py:47
  213.4 4.4 %collective-permute-done.1 = f32[128,512]{1,0:T(8,128)S(1)} collective-permute-done((f32[128,512]{1,0:T(8,128)}, f32[128,512]{1,0:T(8,128)S(1)}, u32[]{:S(2)}, u32[]{:S(2)}) %collective-permute-start.1) | collective-permute-done | bytes 262176 | tf_op jit(solution)/shard_map/while/body/eval_jaxpr/ppermute | solution.py:14
  217.9 1.6 fusion.14
  219.9 1.5 fusion.19
  221.5 7.0 %collective-permute-done.2 = f32[128,512]{1,0:T(8,128)S(1)} collective-permute-done((f32[128,512]{1,0:T(8,128)S(1)}, f32[128,512]{1,0:T(8,128)S(1)}, u32[]{:S(2)}, u32[]{:S(2)}) %collective-permute-start.2) | collective-permute-done | bytes 262176 | tf_op jit(solution)/shard_map/ppermute | solution.py:14
  229.2 2.9 %scatter_fusion.1 = f32[8,128,512]{2,1,0:T(8,128)S(1)} fusion(f32[8,128,512]{2,1,0:T(8,128)S(1)} %copy-done, s32[6]{0:T(128)S(1)} %fusion.22, f32[6,128,512]{2,1,0:T(8,128)} %fusion.19), kind=kCustom, calls=%fused_computation.3 | custom fusion | flops 393216 | bytes 4718616 | tf_op jit(solution)/shard_map/scatter-add | solution.py:47
  232.1 1.7 convert_subtract_fusion
  233.8 5.0 %reduce-scatter.2.cloned.1.call-done = f32[64,512]{1,0:T(8,128)} async-done(((f32[128,512]{1,0:T(8,128)}), f32[64,512]{1,0:T(8,128)}) %reduce-scatter.2.cloned.1.call-update) | async-done | bytes 131088 | tf_op jit(solution)/shard_map/reduce_scatter | solution.py:70
  238.7 1.6 fusion.18
  (212 shorter events, 67.0 us)
Async XLA Ops:
  7.2 231.6 %reduce-scatter.2.cloned.1.call-start = ((), (), s32[]{:S(2)}) async-start(), calls=%async_computation.1 | async-start | bytes 393216 | tf_op jit(solution)/shard_map/reduce_scatter | solution.py:70
  7.2 14.2 %copy-start.1 = (bf16[1024,512]{1,0:T(8,128)(2,1)S(1)}, bf16[1024,512]{1,0:T(8,128)(2,1)}, u32[]{:S(2)}) copy-start(bf16[1024,512]{1,0:T(8,128)(2,1)} %param.9) | copy-start | bytes 3145732
  7.2 14.2 %copy-start.5 = (s32[1,16]{1,0:T(1,128)S(1)}, s32[1,16]{1,0:T(1,128)}, u32[]{:S(2)}) copy-start(s32[1,16]{1,0:T(1,128)} %param.13) | copy-start | bytes 196
  21.4 10.7 %collective-permute-start = (bf16[128,512]{1,0:T(8,128)(2,1)S(1)}, bf16[128,512]{1,0:T(8,128)(2,1)S(1)}, u32[]{:S(2)}, u32[]{:S(2)}) collective-permute-start(bf16[128,512]{1,0:T(8,128)(2,1)S(1)} %copy.22), channel_id=1, source_target_pairs={{0,1},{1,2},{2,3},{3,4},{4,5},{5,6},{6,7},{7,8},{8,9},{9,10},{10,1... | collective-permute-start | bytes 393224 | tf_op jit(solution)/shard_map/while/body/eval_jaxpr/ppermute | solution.py:14
  25.8 8.7 %collective-permute-start.1 = (f32[128,512]{1,0:T(8,128)}, f32[128,512]{1,0:T(8,128)S(1)}, u32[]{:S(2)}, u32[]{:S(2)}) collective-permute-start(f32[128,512]{1,0:T(8,128)} %fusion.42), channel_id=1, source_target_pairs={{0,1},{1,2},{2,3},{3,4},{4,5},{5,6},{6,7},{7,8},{8,9},{9,10},{10,1... | collective-permute-start | bytes 786440 | tf_op jit(solution)/shard_map/while/body/eval_jaxpr/ppermute | solution.py:14
  34.5 8.7 %collective-permute-start = (bf16[128,512]{1,0:T(8,128)(2,1)S(1)}, bf16[128,512]{1,0:T(8,128)(2,1)S(1)}, u32[]{:S(2)}, u32[]{:S(2)}) collective-permute-start(bf16[128,512]{1,0:T(8,128)(2,1)S(1)} %copy.22), channel_id=1, source_target_pairs={{0,1},{1,2},{2,3},{3,4},{4,5},{5,6},{6,7},{7,8},{8,9},{9,10},{10,1... | collective-permute-start | bytes 393224 | tf_op jit(solution)/shard_map/while/body/eval_jaxpr/ppermute | solution.py:14
  38.9 8.7 %collective-permute-start.1 = (f32[128,512]{1,0:T(8,128)}, f32[128,512]{1,0:T(8,128)S(1)}, u32[]{:S(2)}, u32[]{:S(2)}) collective-permute-start(f32[128,512]{1,0:T(8,128)} %fusion.42), channel_id=1, source_target_pairs={{0,1},{1,2},{2,3},{3,4},{4,5},{5,6},{6,7},{7,8},{8,9},{9,10},{10,1... | collective-permute-start | bytes 786440 | tf_op jit(solution)/shard_map/while/body/eval_jaxpr/ppermute | solution.py:14
  47.6 8.6 %collective-permute-start = (bf16[128,512]{1,0:T(8,128)(2,1)S(1)}, bf16[128,512]{1,0:T(8,128)(2,1)S(1)}, u32[]{:S(2)}, u32[]{:S(2)}) collective-permute-start(bf16[128,512]{1,0:T(8,128)(2,1)S(1)} %copy.22), channel_id=1, source_target_pairs={{0,1},{1,2},{2,3},{3,4},{4,5},{5,6},{6,7},{7,8},{8,9},{9,10},{10,1... | collective-permute-start | bytes 393224 | tf_op jit(solution)/shard_map/while/body/eval_jaxpr/ppermute | solution.py:14
  52.0 8.7 %collective-permute-start.1 = (f32[128,512]{1,0:T(8,128)}, f32[128,512]{1,0:T(8,128)S(1)}, u32[]{:S(2)}, u32[]{:S(2)}) collective-permute-start(f32[128,512]{1,0:T(8,128)} %fusion.42), channel_id=1, source_target_pairs={{0,1},{1,2},{2,3},{3,4},{4,5},{5,6},{6,7},{7,8},{8,9},{9,10},{10,1... | collective-permute-start | bytes 786440 | tf_op jit(solution)/shard_map/while/body/eval_jaxpr/ppermute | solution.py:14
  60.7 8.6 %collective-permute-start = (bf16[128,512]{1,0:T(8,128)(2,1)S(1)}, bf16[128,512]{1,0:T(8,128)(2,1)S(1)}, u32[]{:S(2)}, u32[]{:S(2)}) collective-permute-start(bf16[128,512]{1,0:T(8,128)(2,1)S(1)} %copy.22), channel_id=1, source_target_pairs={{0,1},{1,2},{2,3},{3,4},{4,5},{5,6},{6,7},{7,8},{8,9},{9,10},{10,1... | collective-permute-start | bytes 393224 | tf_op jit(solution)/shard_map/while/body/eval_jaxpr/ppermute | solution.py:14
  65.1 8.7 %collective-permute-start.1 = (f32[128,512]{1,0:T(8,128)}, f32[128,512]{1,0:T(8,128)S(1)}, u32[]{:S(2)}, u32[]{:S(2)}) collective-permute-start(f32[128,512]{1,0:T(8,128)} %fusion.42), channel_id=1, source_target_pairs={{0,1},{1,2},{2,3},{3,4},{4,5},{5,6},{6,7},{7,8},{8,9},{9,10},{10,1... | collective-permute-start | bytes 786440 | tf_op jit(solution)/shard_map/while/body/eval_jaxpr/ppermute | solution.py:14
  73.8 8.7 %collective-permute-start = (bf16[128,512]{1,0:T(8,128)(2,1)S(1)}, bf16[128,512]{1,0:T(8,128)(2,1)S(1)}, u32[]{:S(2)}, u32[]{:S(2)}) collective-permute-start(bf16[128,512]{1,0:T(8,128)(2,1)S(1)} %copy.22), channel_id=1, source_target_pairs={{0,1},{1,2},{2,3},{3,4},{4,5},{5,6},{6,7},{7,8},{8,9},{9,10},{10,1... | collective-permute-start | bytes 393224 | tf_op jit(solution)/shard_map/while/body/eval_jaxpr/ppermute | solution.py:14
  78.2 8.7 %collective-permute-start.1 = (f32[128,512]{1,0:T(8,128)}, f32[128,512]{1,0:T(8,128)S(1)}, u32[]{:S(2)}, u32[]{:S(2)}) collective-permute-start(f32[128,512]{1,0:T(8,128)} %fusion.42), channel_id=1, source_target_pairs={{0,1},{1,2},{2,3},{3,4},{4,5},{5,6},{6,7},{7,8},{8,9},{9,10},{10,1... | collective-permute-start | bytes 786440 | tf_op jit(solution)/shard_map/while/body/eval_jaxpr/ppermute | solution.py:14
  86.9 8.6 %collective-permute-start = (bf16[128,512]{1,0:T(8,128)(2,1)S(1)}, bf16[128,512]{1,0:T(8,128)(2,1)S(1)}, u32[]{:S(2)}, u32[]{:S(2)}) collective-permute-start(bf16[128,512]{1,0:T(8,128)(2,1)S(1)} %copy.22), channel_id=1, source_target_pairs={{0,1},{1,2},{2,3},{3,4},{4,5},{5,6},{6,7},{7,8},{8,9},{9,10},{10,1... | collective-permute-start | bytes 393224 | tf_op jit(solution)/shard_map/while/body/eval_jaxpr/ppermute | solution.py:14
  91.3 8.7 %collective-permute-start.1 = (f32[128,512]{1,0:T(8,128)}, f32[128,512]{1,0:T(8,128)S(1)}, u32[]{:S(2)}, u32[]{:S(2)}) collective-permute-start(f32[128,512]{1,0:T(8,128)} %fusion.42), channel_id=1, source_target_pairs={{0,1},{1,2},{2,3},{3,4},{4,5},{5,6},{6,7},{7,8},{8,9},{9,10},{10,1... | collective-permute-start | bytes 786440 | tf_op jit(solution)/shard_map/while/body/eval_jaxpr/ppermute | solution.py:14
  100.0 8.6 %collective-permute-start = (bf16[128,512]{1,0:T(8,128)(2,1)S(1)}, bf16[128,512]{1,0:T(8,128)(2,1)S(1)}, u32[]{:S(2)}, u32[]{:S(2)}) collective-permute-start(bf16[128,512]{1,0:T(8,128)(2,1)S(1)} %copy.22), channel_id=1, source_target_pairs={{0,1},{1,2},{2,3},{3,4},{4,5},{5,6},{6,7},{7,8},{8,9},{9,10},{10,1... | collective-permute-start | bytes 393224 | tf_op jit(solution)/shard_map/while/body/eval_jaxpr/ppermute | solution.py:14
  104.4 8.7 %collective-permute-start.1 = (f32[128,512]{1,0:T(8,128)}, f32[128,512]{1,0:T(8,128)S(1)}, u32[]{:S(2)}, u32[]{:S(2)}) collective-permute-start(f32[128,512]{1,0:T(8,128)} %fusion.42), channel_id=1, source_target_pairs={{0,1},{1,2},{2,3},{3,4},{4,5},{5,6},{6,7},{7,8},{8,9},{9,10},{10,1... | collective-permute-start | bytes 786440 | tf_op jit(solution)/shard_map/while/body/eval_jaxpr/ppermute | solution.py:14
  113.1 8.6 %collective-permute-start = (bf16[128,512]{1,0:T(8,128)(2,1)S(1)}, bf16[128,512]{1,0:T(8,128)(2,1)S(1)}, u32[]{:S(2)}, u32[]{:S(2)}) collective-permute-start(bf16[128,512]{1,0:T(8,128)(2,1)S(1)} %copy.22), channel_id=1, source_target_pairs={{0,1},{1,2},{2,3},{3,4},{4,5},{5,6},{6,7},{7,8},{8,9},{9,10},{10,1... | collective-permute-start | bytes 393224 | tf_op jit(solution)/shard_map/while/body/eval_jaxpr/ppermute | solution.py:14
  117.5 8.7 %collective-permute-start.1 = (f32[128,512]{1,0:T(8,128)}, f32[128,512]{1,0:T(8,128)S(1)}, u32[]{:S(2)}, u32[]{:S(2)}) collective-permute-start(f32[128,512]{1,0:T(8,128)} %fusion.42), channel_id=1, source_target_pairs={{0,1},{1,2},{2,3},{3,4},{4,5},{5,6},{6,7},{7,8},{8,9},{9,10},{10,1... | collective-permute-start | bytes 786440 | tf_op jit(solution)/shard_map/while/body/eval_jaxpr/ppermute | solution.py:14
  126.2 8.6 %collective-permute-start = (bf16[128,512]{1,0:T(8,128)(2,1)S(1)}, bf16[128,512]{1,0:T(8,128)(2,1)S(1)}, u32[]{:S(2)}, u32[]{:S(2)}) collective-permute-start(bf16[128,512]{1,0:T(8,128)(2,1)S(1)} %copy.22), channel_id=1, source_target_pairs={{0,1},{1,2},{2,3},{3,4},{4,5},{5,6},{6,7},{7,8},{8,9},{9,10},{10,1... | collective-permute-start | bytes 393224 | tf_op jit(solution)/shard_map/while/body/eval_jaxpr/ppermute | solution.py:14
  130.6 8.7 %collective-permute-start.1 = (f32[128,512]{1,0:T(8,128)}, f32[128,512]{1,0:T(8,128)S(1)}, u32[]{:S(2)}, u32[]{:S(2)}) collective-permute-start(f32[128,512]{1,0:T(8,128)} %fusion.42), channel_id=1, source_target_pairs={{0,1},{1,2},{2,3},{3,4},{4,5},{5,6},{6,7},{7,8},{8,9},{9,10},{10,1... | collective-permute-start | bytes 786440 | tf_op jit(solution)/shard_map/while/body/eval_jaxpr/ppermute | solution.py:14
  139.3 8.6 %collective-permute-start = (bf16[128,512]{1,0:T(8,128)(2,1)S(1)}, bf16[128,512]{1,0:T(8,128)(2,1)S(1)}, u32[]{:S(2)}, u32[]{:S(2)}) collective-permute-start(bf16[128,512]{1,0:T(8,128)(2,1)S(1)} %copy.22), channel_id=1, source_target_pairs={{0,1},{1,2},{2,3},{3,4},{4,5},{5,6},{6,7},{7,8},{8,9},{9,10},{10,1... | collective-permute-start | bytes 393224 | tf_op jit(solution)/shard_map/while/body/eval_jaxpr/ppermute | solution.py:14
  143.7 8.7 %collective-permute-start.1 = (f32[128,512]{1,0:T(8,128)}, f32[128,512]{1,0:T(8,128)S(1)}, u32[]{:S(2)}, u32[]{:S(2)}) collective-permute-start(f32[128,512]{1,0:T(8,128)} %fusion.42), channel_id=1, source_target_pairs={{0,1},{1,2},{2,3},{3,4},{4,5},{5,6},{6,7},{7,8},{8,9},{9,10},{10,1... | collective-permute-start | bytes 786440 | tf_op jit(solution)/shard_map/while/body/eval_jaxpr/ppermute | solution.py:14
  152.4 8.6 %collective-permute-start = (bf16[128,512]{1,0:T(8,128)(2,1)S(1)}, bf16[128,512]{1,0:T(8,128)(2,1)S(1)}, u32[]{:S(2)}, u32[]{:S(2)}) collective-permute-start(bf16[128,512]{1,0:T(8,128)(2,1)S(1)} %copy.22), channel_id=1, source_target_pairs={{0,1},{1,2},{2,3},{3,4},{4,5},{5,6},{6,7},{7,8},{8,9},{9,10},{10,1... | collective-permute-start | bytes 393224 | tf_op jit(solution)/shard_map/while/body/eval_jaxpr/ppermute | solution.py:14
  156.8 8.7 %collective-permute-start.1 = (f32[128,512]{1,0:T(8,128)}, f32[128,512]{1,0:T(8,128)S(1)}, u32[]{:S(2)}, u32[]{:S(2)}) collective-permute-start(f32[128,512]{1,0:T(8,128)} %fusion.42), channel_id=1, source_target_pairs={{0,1},{1,2},{2,3},{3,4},{4,5},{5,6},{6,7},{7,8},{8,9},{9,10},{10,1... | collective-permute-start | bytes 786440 | tf_op jit(solution)/shard_map/while/body/eval_jaxpr/ppermute | solution.py:14
  165.5 8.7 %collective-permute-start = (bf16[128,512]{1,0:T(8,128)(2,1)S(1)}, bf16[128,512]{1,0:T(8,128)(2,1)S(1)}, u32[]{:S(2)}, u32[]{:S(2)}) collective-permute-start(bf16[128,512]{1,0:T(8,128)(2,1)S(1)} %copy.22), channel_id=1, source_target_pairs={{0,1},{1,2},{2,3},{3,4},{4,5},{5,6},{6,7},{7,8},{8,9},{9,10},{10,1... | collective-permute-start | bytes 393224 | tf_op jit(solution)/shard_map/while/body/eval_jaxpr/ppermute | solution.py:14
  169.9 8.7 %collective-permute-start.1 = (f32[128,512]{1,0:T(8,128)}, f32[128,512]{1,0:T(8,128)S(1)}, u32[]{:S(2)}, u32[]{:S(2)}) collective-permute-start(f32[128,512]{1,0:T(8,128)} %fusion.42), channel_id=1, source_target_pairs={{0,1},{1,2},{2,3},{3,4},{4,5},{5,6},{6,7},{7,8},{8,9},{9,10},{10,1... | collective-permute-start | bytes 786440 | tf_op jit(solution)/shard_map/while/body/eval_jaxpr/ppermute | solution.py:14
  178.6 8.7 %collective-permute-start = (bf16[128,512]{1,0:T(8,128)(2,1)S(1)}, bf16[128,512]{1,0:T(8,128)(2,1)S(1)}, u32[]{:S(2)}, u32[]{:S(2)}) collective-permute-start(bf16[128,512]{1,0:T(8,128)(2,1)S(1)} %copy.22), channel_id=1, source_target_pairs={{0,1},{1,2},{2,3},{3,4},{4,5},{5,6},{6,7},{7,8},{8,9},{9,10},{10,1... | collective-permute-start | bytes 393224 | tf_op jit(solution)/shard_map/while/body/eval_jaxpr/ppermute | solution.py:14
  183.0 8.7 %collective-permute-start.1 = (f32[128,512]{1,0:T(8,128)}, f32[128,512]{1,0:T(8,128)S(1)}, u32[]{:S(2)}, u32[]{:S(2)}) collective-permute-start(f32[128,512]{1,0:T(8,128)} %fusion.42), channel_id=1, source_target_pairs={{0,1},{1,2},{2,3},{3,4},{4,5},{5,6},{6,7},{7,8},{8,9},{9,10},{10,1... | collective-permute-start | bytes 786440 | tf_op jit(solution)/shard_map/while/body/eval_jaxpr/ppermute | solution.py:14
  191.7 8.7 %collective-permute-start = (bf16[128,512]{1,0:T(8,128)(2,1)S(1)}, bf16[128,512]{1,0:T(8,128)(2,1)S(1)}, u32[]{:S(2)}, u32[]{:S(2)}) collective-permute-start(bf16[128,512]{1,0:T(8,128)(2,1)S(1)} %copy.22), channel_id=1, source_target_pairs={{0,1},{1,2},{2,3},{3,4},{4,5},{5,6},{6,7},{7,8},{8,9},{9,10},{10,1... | collective-permute-start | bytes 393224 | tf_op jit(solution)/shard_map/while/body/eval_jaxpr/ppermute | solution.py:14
  196.1 8.7 %collective-permute-start.1 = (f32[128,512]{1,0:T(8,128)}, f32[128,512]{1,0:T(8,128)S(1)}, u32[]{:S(2)}, u32[]{:S(2)}) collective-permute-start(f32[128,512]{1,0:T(8,128)} %fusion.42), channel_id=1, source_target_pairs={{0,1},{1,2},{2,3},{3,4},{4,5},{5,6},{6,7},{7,8},{8,9},{9,10},{10,1... | collective-permute-start | bytes 786440 | tf_op jit(solution)/shard_map/while/body/eval_jaxpr/ppermute | solution.py:14
  204.8 8.6 %collective-permute-start = (bf16[128,512]{1,0:T(8,128)(2,1)S(1)}, bf16[128,512]{1,0:T(8,128)(2,1)S(1)}, u32[]{:S(2)}, u32[]{:S(2)}) collective-permute-start(bf16[128,512]{1,0:T(8,128)(2,1)S(1)} %copy.22), channel_id=1, source_target_pairs={{0,1},{1,2},{2,3},{3,4},{4,5},{5,6},{6,7},{7,8},{8,9},{9,10},{10,1... | collective-permute-start | bytes 393224 | tf_op jit(solution)/shard_map/while/body/eval_jaxpr/ppermute | solution.py:14
  209.1 8.7 %collective-permute-start.1 = (f32[128,512]{1,0:T(8,128)}, f32[128,512]{1,0:T(8,128)S(1)}, u32[]{:S(2)}, u32[]{:S(2)}) collective-permute-start(f32[128,512]{1,0:T(8,128)} %fusion.42), channel_id=1, source_target_pairs={{0,1},{1,2},{2,3},{3,4},{4,5},{5,6},{6,7},{7,8},{8,9},{9,10},{10,1... | collective-permute-start | bytes 786440 | tf_op jit(solution)/shard_map/while/body/eval_jaxpr/ppermute | solution.py:14
  217.9 1.7 copy-start.2
  219.5 9.7 %copy-start = (f32[8,128,512]{2,1,0:T(8,128)S(1)}, f32[8,128,512]{2,1,0:T(8,128)}, u32[]{:S(2)}) copy-start(f32[8,128,512]{2,1,0:T(8,128)} %get-tuple-element.248) | copy-start | bytes 6291460
  219.9 8.5 %collective-permute-start.2 = (f32[128,512]{1,0:T(8,128)S(1)}, f32[128,512]{1,0:T(8,128)S(1)}, u32[]{:S(2)}, u32[]{:S(2)}) collective-permute-start(f32[128,512]{1,0:T(8,128)S(1)} %fusion.15), channel_id=1, source_target_pairs={{0,1},{1,2},{2,3},{3,4},{4,5},{5,6},{6,7},{7,8},{8,9},{9,10},{10,1... | collective-permute-start | bytes 786440 | tf_op jit(solution)/shard_map/ppermute | solution.py:14
  228.4 0.7 copy-start.4
  232.1 6.7 %copy-start.3 = (bf16[1,64,512]{2,1,0:T(8,128)(2,1)S(1)}, bf16[1,64,512]{2,1,0:T(8,128)(2,1)}, u32[]{:S(2)}) copy-start(bf16[1,64,512]{2,1,0:T(8,128)(2,1)} %param.10) | copy-start | bytes 196612
Sparse Core Ops, SparseCore 0:
  229.3 9.4 reduce-scatter.1
where the time goes:
time: 248 us; the launch traced here: 247 us
  waiting for transfers between devices  76.4 us (31%)
  other arithmetic  75.5 us (30%)
  matrix products  44.3 us (18%)
  local copies, waits for them, and re-layouts  26.3 us (11%)
  between operations  14.2 us (6%)
  blocking collectives  6.11 us (2%)
  starting transfers between devices  3.08 us (1%)
    ppermute x31, waiting for transfers between devices, passed_along(): return lax.ppermute(value, axis, pairs)  71.4 us
    scatter-add x16, other arithmetic, padded_work(): region_totals = region_totals.at[rows_now].add(update)  61.4 us
    dot_general x16, matrix products, padded_work(): jnp.einsum('sik,jk->sij', chosen, panel_now, preferred_element_type=jnp.f...  21.7 us
    dot_general x16, matrix products, padded_work(): jnp.einsum('sij,sik->jk', residual, chosen, preferred_element_type=jnp.fl...  16 us
    gather x16, local copies, waits for them, and re-layouts, padded_work(): chosen = jnp.take(region_blocks, rows_now, axis=0)  11.7 us
    dynamic_slice x16, local copies, waits for them, and re-layouts, padded_work(): count_now = lax.dynamic_index_in_dim(live_counts, column, 0, keepdims=False)  10.4 us
    lt x15, other arithmetic, padded_work(): present = slot_ids < count_now  9.58 us
    dot_general x16, matrix products, padded_work(): jnp.einsum('sij,jk->sik', residual, panel_now, preferred_element_type=jnp...  6.59 us
  transfers between devices with their start and end apart: 32, of which 17 were waited for; matrix products, arithmetic and copies ran while one was open for 54% of the time, Pallas kernels for 0%

commit v1 on v0

v1 whole, which is shorter than its diff:
```python
import functools

import jax
import jax.numpy as jnp
from jax import lax
from jax.experimental import pallas as pl
from jax.experimental.pallas import tpu as pltpu
from jax.sharding import PartitionSpec as P

region_rate = 0.05
item_rate = 0.01
decay_rate = 0.1

MESH = pl.DeviceIdType.MESH
CORES = 2
NT = (((1,), (1,)), ((), ()))
TN = (((0,), (0,)), ((), ()))
NN = (((1,), (0,)), ((), ()))


def mm(a, b, dims):
    return lax.dot_general(a, b, dims, preferred_element_type=jnp.float32)


def kernel(R, Z, Y, chunk, items, regions, slab, rows, counts, new_regions, new_items,
           u, tiles, v, res, racc, gown, gsend, grecv,
           s_a, r_a, s_b, r_b, s_x, r_x, s_y, r_y, s_z, r_z, acc,
           loc_sem, out_sem, az, ax, ay, aa, ab, sib, gc, ga, gb, gx, gy, gz):
    x = lax.axis_index("row")
    c = lax.axis_index("col")
    k = lax.rem(c, CORES)
    y = lax.rem(c // CORES, Y)
    z = c // (CORES * Y)
    block = tiles.shape[-1]
    width = u.shape[-1]
    half = width // 2
    n = block // R
    slots = tiles.shape[1]
    chunks = u.shape[0] // chunk

    def col_of(zz, yy, kk):
        return (zz * Y + yy) * CORES + kk

    def xdev(d):
        return {"row": lax.rem(x + d, R), "col": c}

    def ydev(d):
        return {"row": x, "col": col_of(z, lax.rem(y + d, Y), k)}

    def zdev(d):
        return {"row": x, "col": col_of(lax.rem(z + d, Z), y, k)}

    sibling = {"row": x, "col": col_of(z, y, 1 - k)}
    peers = [xdev(d) for d in range(1, R)] + [ydev(d) for d in range(1, Y)] + [zdev(d) for d in range(1, Z)] + [sibling]

    load_u = pltpu.make_async_copy(regions, u, loc_sem.at[0])
    load_u.start()
    load_tiles = pltpu.make_async_copy(slab.at[0], tiles, loc_sem.at[1])
    load_tiles.start()

    barrier = pltpu.get_barrier_semaphore()
    for peer in peers:
        pl.semaphore_signal(barrier, inc=1, device_id=peer, device_id_type=MESH)
    pl.semaphore_wait(barrier, len(peers))

    sent = []

    def remote(src, dst, sems, index, device):
        return pltpu.make_async_remote_copy(
            src_ref=src, dst_ref=dst, send_sem=sems.at[(0,) + index], recv_sem=sems.at[(1,) + index],
            device_id=device, device_id_type=MESH)

    def send(src, dst, sems, index, device):
        copy = remote(src, dst, sems, index, device)
        copy.start()
        sent.append(copy)

    def arrived(dst, sems, index):
        remote(dst, dst, sems, index, sibling).wait_recv()

    def zslot(j):
        return lax.rem(z + j, Z)

    def xback(d):
        return lax.rem(x + R - d, R)

    def yback(d):
        return lax.rem(y + Y - d, Y)

    def at_row(yy, xx):
        return pl.ds(pl.multiple_of(yy * block + xx * n, n), n)

    def piece(j, yy, xx, columns=slice(None)):
        return v.at[zslot(j), k, at_row(yy, xx), columns]

    first, second = pl.ds(0, half), pl.ds(half, half)

    def plane_start(j):
        own = piece(j, y, x)
        for d in range(1, R):
            send(own, own, ax, (j, d), xdev(d))
        for d in range(1, Y):
            send(own, own, ay, (j, d), ydev(d))

    def forward(j):
        for dx in range(1, R):
            arrived(piece(j, y, xback(dx)), ax, (j, dx))
            part = piece(j, y, xback(dx), first)
            for dy in range(1, Y):
                send(part, part, aa, (j, dx, dy), ydev(dy))
        for dy in range(1, Y):
            arrived(piece(j, yback(dy), x), ay, (j, dy))
            part = piece(j, yback(dy), x, second)
            for dx in range(1, R):
                send(part, part, ab, (j, dx, dy), xdev(dx))

    def share(j):
        for dx in range(1, R):
            for dy in range(1, Y):
                arrived(piece(j, yback(dy), xback(dx), first), aa, (j, dx, dy))
                arrived(piece(j, yback(dy), xback(dx), second), ab, (j, dx, dy))
        mine = v.at[zslot(j), k]
        send(mine, mine, sib, (j,), sibling)

    def shared(j):
        arrived(v.at[zslot(j), 1 - k], sib, (j,))

    def residuals(j):
        zz = zslot(j)

        def body(i, carry):
            start = pl.multiple_of(i * chunk, chunk)
            u_now = u[pl.ds(start, chunk), :]
            for o in range(CORES):
                kk = lax.rem(k + o, CORES)
                predicted = mm(u_now, v[zz, kk], NT)
                for yy in range(Y):
                    p = col_of(zz, yy, kk)
                    count = counts[0, p]
                    for part in range(chunk // block):
                        b = i * (chunk // block) + part
                        found = jnp.int32(0)
                        for s in range(slots):
                            hit = (rows[0, p, s] == b) & (count > s)
                            found = jnp.where(hit, s + 1, found)
                        live = jnp.where(found > 0, jnp.float32(1), jnp.float32(0))
                        tile = tiles[p, jnp.maximum(found - 1, 0)].astype(jnp.float32)
                        pred = predicted[part * block:(part + 1) * block, yy * block:(yy + 1) * block]
                        res[o, pl.ds(pl.multiple_of(start + part * block, block), block), yy * block:(yy + 1) * block] = (
                            (pred - tile) * live).astype(jnp.bfloat16)
            return carry

        lax.fori_loop(0, chunks, body, 0)

    def region_part(j):
        zz = zslot(j)

        def body(i, carry):
            here = pl.ds(pl.multiple_of(i * chunk, chunk), chunk)
            total = mm(res[0, here, :], v[zz, k], NN) + mm(res[1, here, :], v[zz, 1 - k], NN)
            if j > 0:
                total = total + racc[here, :]
            if j == Z - 1:
                wide = u[here, :].astype(jnp.float32)
                total = wide - region_rate * (total + decay_rate * wide)
            racc[here, :] = total
            if j == Z - 1:
                pltpu.make_async_copy(racc.at[here, :], new_regions.at[here, :], out_sem.at[i]).start()
            return carry

        lax.fori_loop(0, chunks, body, 0)

    def reduce_first(j):
        arrived(grecv.at[j], gc, (j,))
        gown[j] = gown[j] + grecv[j]
        for dy in range(1, Y):
            yy = lax.rem(y + dy, Y)
            for dx in range(1, R):
                s_a[j, dy - 1, (dx - 1) * n:dx * n, :] = gown[j, at_row(yy, lax.rem(x + dx, R)), :half].astype(jnp.bfloat16)
            send(s_a.at[j, dy - 1], r_a.at[j, dy - 1], ga, (j, dy), ydev(dy))
        for dx in range(1, R):
            xx = lax.rem(x + dx, R)
            for dy in range(1, Y):
                s_b[j, dx - 1, (dy - 1) * n:dy * n, :] = gown[j, at_row(lax.rem(y + dy, Y), xx), half:].astype(jnp.bfloat16)
            send(s_b.at[j, dx - 1], r_b.at[j, dx - 1], gb, (j, dx), xdev(dx))

    def reduce_second(j):
        for dy in range(1, Y):
            arrived(r_a.at[j, dy - 1], ga, (j, dy))
        for dx in range(1, R):
            here = at_row(y, lax.rem(x + dx, R))
            total = gown[j, here, :half]
            for dy in range(1, Y):
                total = total + r_a[j, dy - 1, (dx - 1) * n:dx * n, :].astype(jnp.float32)
            s_x[j, dx - 1, :, :half] = total.astype(jnp.bfloat16)
            s_x[j, dx - 1, :, half:] = gown[j, here, half:].astype(jnp.bfloat16)
            send(s_x.at[j, dx - 1], r_x.at[j, dx - 1], gx, (j, dx), xdev(dx))
        for dx in range(1, R):
            arrived(r_b.at[j, dx - 1], gb, (j, dx))
        for dy in range(1, Y):
            here = at_row(lax.rem(y + dy, Y), x)
            total = gown[j, here, half:]
            for dx in range(1, R):
                total = total + r_b[j, dx - 1, (dy - 1) * n:dy * n, :].astype(jnp.float32)
            s_y[j, dy - 1, :, half:] = total.astype(jnp.bfloat16)
            s_y[j, dy - 1, :, :half] = gown[j, here, :half].astype(jnp.bfloat16)
            send(s_y.at[j, dy - 1], r_y.at[j, dy - 1], gy, (j, dy), ydev(dy))

    def reduce_third(j):
        total = gown[j, at_row(y, x), :]
        for dx in range(1, R):
            arrived(r_x.at[j, dx - 1], gx, (j, dx))
            total = total + r_x[j, dx - 1].astype(jnp.float32)
        for dy in range(1, Y):
            arrived(r_y.at[j, dy - 1], gy, (j, dy))
            total = total + r_y[j, dy - 1].astype(jnp.float32)
        if j == 0:
            acc[...] = total
        else:
            s_z[j - 1] = total.astype(jnp.bfloat16)
            send(s_z.at[j - 1], r_z.at[j - 1], gz, (j,), zdev(j))

    v[z, k, at_row(y, x), :] = items[0]
    own = piece(0, y, x)
    plane_start(0)
    for d in range(1, Z):
        send(own, own, az, (d,), zdev(d))
    for j in range(1, Z):
        arrived(piece(j, y, x), az, (Z - j,))
        plane_start(j)
    forward(0)
    for j in range(Z):
        if j + 1 < Z:
            forward(j + 1)
        share(j)
        shared(j)
        if j == 0:
            load_u.wait()
            load_tiles.wait()
        residuals(j)
        gsend[j] = mm(res[1], u[...], TN)
        send(gsend.at[j], grecv.at[j], gc, (j,), sibling)
        if j > 0:
            reduce_second(j - 1)
        gown[j] = mm(res[0], u[...], TN)
        region_part(j)
        reduce_first(j)
        if j > 0:
            reduce_third(j - 1)
    reduce_second(Z - 1)
    reduce_third(Z - 1)
    total = acc[...]
    for j in range(1, Z):
        arrived(r_z.at[j - 1], gz, (j,))
        total = total + r_z[j - 1].astype(jnp.float32)
    wide = items[0].astype(jnp.float32)
    new_items[0] = wide - item_rate * (total + decay_rate * wide)
    for copy in sent:
        copy.wait_send()

    def finish(i, carry):
        here = pl.ds(pl.multiple_of(i * chunk, chunk), chunk)
        pltpu.make_async_copy(racc.at[here, :], new_regions.at[here, :], out_sem.at[i]).wait()
        return carry

    lax.fori_loop(0, chunks, finish, 0)


def on_device(R, Z, Y, region_factors, item_factors, slab_blocks, block_rows, counts):
    bf16, f32 = jnp.bfloat16, jnp.float32
    height, width = region_factors.shape
    _, panels, slots, block, _ = slab_blocks.shape
    n, half, side = block // R, width // 2, Y * block
    chunk = 2 * block
    dma = pltpu.SemaphoreType.DMA
    vmem = pltpu.VMEM
    return pl.pallas_call(
        functools.partial(kernel, R, Z, Y, chunk),
        out_shape=(jax.ShapeDtypeStruct((height, width), f32), jax.ShapeDtypeStruct(item_factors.shape, f32)),
        in_specs=[
            pl.BlockSpec(memory_space=pltpu.VMEM),
            pl.BlockSpec(memory_space=pl.ANY),
            pl.BlockSpec(memory_space=pl.ANY),
            pl.BlockSpec(memory_space=pltpu.SMEM),
            pl.BlockSpec(memory_space=pltpu.SMEM),
        ],
        out_specs=(pl.BlockSpec(memory_space=pl.ANY), pl.BlockSpec(memory_space=pltpu.VMEM)),
        scratch_shapes=[
            vmem((height, width), bf16),
            vmem((panels, slots, block, block), bf16),
            vmem((Z, CORES, side, width), bf16),
            vmem((CORES, height, side), bf16),
            vmem((height, width), f32),
            vmem((Z, side, width), f32),
            vmem((Z, side, width), f32),
            vmem((Z, side, width), f32),
            vmem((Z, Y - 1, (R - 1) * n, half), bf16),
            vmem((Z, Y - 1, (R - 1) * n, half), bf16),
            vmem((Z, R - 1, (Y - 1) * n, half), bf16),
            vmem((Z, R - 1, (Y - 1) * n, half), bf16),
            vmem((Z, R - 1, n, width), bf16),
            vmem((Z, R - 1, n, width), bf16),
            vmem((Z, Y - 1, n, width), bf16),
            vmem((Z, Y - 1, n, width), bf16),
            vmem((Z - 1, n, width), bf16),
            vmem((Z - 1, n, width), bf16),
            vmem((n, width), f32),
            dma((2,)),
            dma((height // chunk,)),
            dma((2, Z)),
            dma((2, Z, R)),
            dma((2, Z, Y)),
            dma((2, Z, R, Y)),
            dma((2, Z, R, Y)),
            dma((2, Z)),
            dma((2, Z)),
            dma((2, Z, Y)),
            dma((2, Z, R)),
            dma((2, Z, R)),
            dma((2, Z, Y)),
            dma((2, Z)),
        ],
        compiler_params=pltpu.CompilerParams(
            collective_id=0, has_side_effects=True, vmem_limit_bytes=56 * 1024 * 1024),
        cost_estimate=pl.CostEstimate(
            flops=6 * height * panels * block * width, bytes_accessed=8 * height * width, transcendentals=0),
    )(item_factors, region_factors, slab_blocks, block_rows, counts)


def solution(mesh):
    R, C = mesh.shape["row"], mesh.shape["col"]
    chips = C // CORES
    Z = 4
    Y = chips // Z
    return jax.shard_map(
        functools.partial(on_device, R, Z, Y),
        mesh=mesh,
        in_specs=(
            P(("row", "col"), None),
            P("col", "row", None),
            P(("row", "col"), None, None, None, None),
            P(("row", "col"), None, None),
            P(("row", "col"), None),
        ),
        out_specs=(P(("row", "col"), None), P("col", "row", None)),
        check_vma=False,
    )
```

time: 248 us -> 60.4 us (0.24)
  waiting for transfers between devices: 76.4 us -> 0 us
  other arithmetic: 75.5 us -> 0 us
  Pallas kernels: 0 us -> 54.4 us
  matrix products: 44.3 us -> 0 us
  local copies, waits for them, and re-layouts: 26.3 us -> 5.13 us
  between operations: 14.2 us -> 0.65 us
  blocking collectives: 6.11 us -> 0 us
  starting transfers between devices: 3.08 us -> 0 us
    ppermute x31 -> x0, waiting for transfers between devices: 71.4 us -> none  [passed_along(): return lax.ppermute(value, axis, pairs)]
    scatter-add x16 -> x0, other arithmetic: 61.4 us -> none  [padded_work(): region_totals = region_totals.at[rows_now].add(update)]
    pallas_call x0 -> x1, Pallas kernels: none -> 54.4 us  [on_device(): pl.pallas_call(functools.partial(kernel, R, Z, Y, chunk), out_shape=(jax....]
    dot_general x48 -> x0, matrix products: 44.3 us -> none  [the longest x16 21.7 us: padded_work(): jnp.einsum('sik,jk->sij', chosen, panel_now, preferred_element_type=jnp.f...]
    gather x16 -> x0, local copies, waits for them, and re-layouts: 11.7 us -> none  [padded_work(): chosen = jnp.take(region_blocks, rows_now, axis=0)]
    dynamic_slice x17 -> x0, local copies, waits for them, and re-layouts: 11.3 us -> none  [the longest x16 10.4 us: padded_work(): count_now = lax.dynamic_index_in_dim(live_counts, column, 0, keepdims=False)]
    lt x15 -> x0, other arithmetic: 9.58 us -> none  [padded_work(): present = slot_ids < count_now]
    all_gather x1 -> x0, blocking collectives: 6.11 us -> none  [on_device(): panel_start = lax.all_gather(item_factors, 'row', axis=1, tiled=True)[0]]
  transfers between devices with their start and end apart: 32 -> 0, of which waited for: 17 -> 0; matrix products, arithmetic and copies ran while one was open for 54% -> 0% of each run, Pallas kernels for 0% -> 0%
where the time goes in v1:
time: 60.4 us; the launch traced here: 60.2 us
  Pallas kernels  54.4 us (90%)
  local copies, waits for them, and re-layouts  5.13 us (8%)
  between operations  0.65 us (1%)
    pallas_call x1, Pallas kernels, on_device(): pl.pallas_call(functools.partial(kernel, R, Z, Y, chunk), out_shape=(jax....  54.4 us
    unnamed x5, local copies, waits for them, and re-layouts  5.13 us

profile of v1, /device:TPU:0, one launch (start us, length us, event | category | flops | bytes accessed | tf_op | source)
XLA Modules:
  0.0 60.2 jit_solution(4513016183591899353)
XLA Ops:
  0.6 1.4 %copy.7.rows = s32[1,16,6]{2,1,0:T(8,128)} copy(s32[1,16,6]{1,0,2:T(1,128)} %param.8) | data formatting | bytes 768 | tf_op args[3]
  2.0 54.4 %shard_map.68 = (f32[1024,512]{1,0:T(8,128)}, f32[1,64,512]{2,1,0:T(8,128)}) custom-call(bf16[1,64,512]{2,1,0:T(8,128)(2,1)} %items.1, bf16[1024,512]{1,0:T(8,128)(2,1)} %regions.1, bf16[1,16,6,128,128]{4,3,2,1,0:T(8,128)(2,1)} %slab.1, s32[1,16,6]{2,1,0:T(8,128)} %copy.7.rows, s32[1,16]{1,0:T(1,128)} %counts.1), custom_call_target="tpu_custom_call" | custom-call | flops 6442450944 | bytes 4194304 | tf_op jit(solution)/shard_map/pallas_call | solution.py:277
  56.4 0.0 copy-start
  56.4 3.1 %copy.10 = f32[1024,512]{1,0:T(8,128)} copy(f32[1024,512]{1,0:T(8,128)} %get-tuple-element.4) | data formatting | bytes 4194304
  59.5 0.0 copy-done
  59.5 0.7 %copy.11 = f32[1,64,512]{2,1,0:T(8,128)} copy(f32[1,64,512]{2,1,0:T(8,128)S(1)} %copy-done) | data formatting | bytes 262144
Async XLA Ops:
  56.4 3.1 %copy-start = (f32[1,64,512]{2,1,0:T(8,128)S(1)}, f32[1,64,512]{2,1,0:T(8,128)}, u32[]{:S(2)}) copy-start(f32[1,64,512]{2,1,0:T(8,128)} %get-tuple-element.5) | copy-start | bytes 393220

commit v2 on v1

--- a/solution.py
+++ b/solution.py
@@ -22,7 +22,7 @@
     return lax.dot_general(a, b, dims, preferred_element_type=jnp.float32)
 
 
-def kernel(R, Z, Y, chunk, items, regions, slab, rows, counts, new_regions, new_items,
+def kernel(R, Z, Y, chunk, items, regions, slab, rows, counts, region_grad, new_items,
            u, tiles, v, res, racc, gown, gsend, grecv,
            s_a, r_a, s_b, r_b, s_x, r_x, s_y, r_y, s_z, r_z, acc,
            loc_sem, out_sem, az, ax, ay, aa, ab, sib, gc, ga, gb, gx, gy, gz):
@@ -87,11 +87,16 @@
     def yback(d):
         return lax.rem(y + Y - d, Y)
 
+    side = Y * block
+
     def at_row(yy, xx):
         return pl.ds(pl.multiple_of(yy * block + xx * n, n), n)
 
+    def core_rows(kk):
+        return pl.ds(pl.multiple_of(kk * side, side), side)
+
     def piece(j, yy, xx, columns=slice(None)):
-        return v.at[zslot(j), k, at_row(yy, xx), columns]
+        return v.at[zslot(j), pl.ds(pl.multiple_of(k * side + yy * block + xx * n, n), n), columns]
 
     first, second = pl.ds(0, half), pl.ds(half, half)
 
@@ -119,34 +124,33 @@
             for dy in range(1, Y):
                 arrived(piece(j, yback(dy), xback(dx), first), aa, (j, dx, dy))
                 arrived(piece(j, yback(dy), xback(dx), second), ab, (j, dx, dy))
-        mine = v.at[zslot(j), k]
+        mine = v.at[zslot(j), core_rows(k)]
         send(mine, mine, sib, (j,), sibling)
 
     def shared(j):
-        arrived(v.at[zslot(j), 1 - k], sib, (j,))
+        arrived(v.at[zslot(j), core_rows(1 - k)], sib, (j,))
 
     def residuals(j):
         zz = zslot(j)
 
         def body(i, carry):
             start = pl.multiple_of(i * chunk, chunk)
-            u_now = u[pl.ds(start, chunk), :]
-            for o in range(CORES):
-                kk = lax.rem(k + o, CORES)
-                predicted = mm(u_now, v[zz, kk], NT)
+            predicted = mm(u[pl.ds(start, chunk), :], v[zz], NT)
+            for kk in range(CORES):
                 for yy in range(Y):
+                    left = (kk * Y + yy) * block
                     p = col_of(zz, yy, kk)
                     count = counts[0, p]
                     for part in range(chunk // block):
                         b = i * (chunk // block) + part
                         found = jnp.int32(0)
                         for s in range(slots):
-                            hit = (rows[0, p, s] == b) & (count > s)
+                            hit = (rows[s, 0, p] == b) & (count > s)
                             found = jnp.where(hit, s + 1, found)
                         live = jnp.where(found > 0, jnp.float32(1), jnp.float32(0))
                         tile = tiles[p, jnp.maximum(found - 1, 0)].astype(jnp.float32)
-                        pred = predicted[part * block:(part + 1) * block, yy * block:(yy + 1) * block]
-                        res[o, pl.ds(pl.multiple_of(start + part * block, block), block), yy * block:(yy + 1) * block] = (
+                        pred = predicted[part * block:(part + 1) * block, left:left + block]
+                        res[pl.ds(pl.multiple_of(start + part * block, block), block), left:left + block] = (
                             (pred - tile) * live).astype(jnp.bfloat16)
             return carry
 
@@ -157,15 +161,12 @@
 
         def body(i, carry):
             here = pl.ds(pl.multiple_of(i * chunk, chunk), chunk)
-            total = mm(res[0, here, :], v[zz, k], NN) + mm(res[1, here, :], v[zz, 1 - k], NN)
+            total = mm(res[here, :], v[zz], NN)
             if j > 0:
                 total = total + racc[here, :]
-            if j == Z - 1:
-                wide = u[here, :].astype(jnp.float32)
-                total = wide - region_rate * (total + decay_rate * wide)
             racc[here, :] = total
             if j == Z - 1:
-                pltpu.make_async_copy(racc.at[here, :], new_regions.at[here, :], out_sem.at[i]).start()
+                pltpu.make_async_copy(racc.at[here, :], region_grad.at[here, :], out_sem.at[i]).start()
             return carry
 
         lax.fori_loop(0, chunks, body, 0)
@@ -220,33 +221,47 @@
             s_z[j - 1] = total.astype(jnp.bfloat16)
             send(s_z.at[j - 1], r_z.at[j - 1], gz, (j,), zdev(j))
 
-    v[z, k, at_row(y, x), :] = items[0]
+    def item_part(kk):
+        return mm(res[:, core_rows(kk)], u[...], TN)
+
+    def plane_next(j):
+        if j < Z:
+            arrived(piece(j, y, x), az, (Z - j,))
+            plane_start(j)
+
+    v[z, pl.ds(pl.multiple_of(k * side + y * block + x * n, n), n), :] = items[0]
     own = piece(0, y, x)
     plane_start(0)
     for d in range(1, Z):
         send(own, own, az, (d,), zdev(d))
-    for j in range(1, Z):
-        arrived(piece(j, y, x), az, (Z - j,))
-        plane_start(j)
     forward(0)
+    plane_next(1)
+    share(0)
+    plane_next(2)
+    shared(0)
+    load_u.wait()
+    load_tiles.wait()
     for j in range(Z):
-        if j + 1 < Z:
+        last = j == Z - 1
+        residuals(j)
+        if not last:
             forward(j + 1)
-        share(j)
-        shared(j)
-        if j == 0:
-            load_u.wait()
-            load_tiles.wait()
-        residuals(j)
-        gsend[j] = mm(res[1], u[...], TN)
-        send(gsend.at[j], grecv.at[j], gc, (j,), sibling)
         if j > 0:
             reduce_second(j - 1)
-        gown[j] = mm(res[0], u[...], TN)
-        region_part(j)
+        gsend[j] = item_part(1 - k)
+        send(gsend.at[j], grecv.at[j], gc, (j,), sibling)
+        if not last:
+            share(j + 1)
+        gown[j] = item_part(k)
+        plane_next(j + 3)
+        if not last:
+            region_part(j)
         reduce_first(j)
         if j > 0:
             reduce_third(j - 1)
+        if not last:
+            shared(j + 1)
+    region_part(Z - 1)
     reduce_second(Z - 1)
     reduce_third(Z - 1)
     total = acc[...]
@@ -260,7 +275,7 @@
 
     def finish(i, carry):
         here = pl.ds(pl.multiple_of(i * chunk, chunk), chunk)
-        pltpu.make_async_copy(racc.at[here, :], new_regions.at[here, :], out_sem.at[i]).wait()
+        pltpu.make_async_copy(racc.at[here, :], region_grad.at[here, :], out_sem.at[i]).wait()
         return carry
 
     lax.fori_loop(0, chunks, finish, 0)
@@ -271,10 +286,10 @@
     height, width = region_factors.shape
     _, panels, slots, block, _ = slab_blocks.shape
     n, half, side = block // R, width // 2, Y * block
-    chunk = 2 * block
+    chunk = 4 * block
     dma = pltpu.SemaphoreType.DMA
     vmem = pltpu.VMEM
-    return pl.pallas_call(
+    region_grad, new_items = pl.pallas_call(
         functools.partial(kernel, R, Z, Y, chunk),
         out_shape=(jax.ShapeDtypeStruct((height, width), f32), jax.ShapeDtypeStruct(item_factors.shape, f32)),
         in_specs=[
@@ -288,8 +303,8 @@
         scratch_shapes=[
             vmem((height, width), bf16),
             vmem((panels, slots, block, block), bf16),
-            vmem((Z, CORES, side, width), bf16),
-            vmem((CORES, height, side), bf16),
+            vmem((Z, CORES * side, width), bf16),
+            vmem((height, CORES * side), bf16),
             vmem((height, width), f32),
             vmem((Z, side, width), f32),
             vmem((Z, side, width), f32),
@@ -324,7 +339,9 @@
             collective_id=0, has_side_effects=True, vmem_limit_bytes=56 * 1024 * 1024),
         cost_estimate=pl.CostEstimate(
             flops=6 * height * panels * block * width, bytes_accessed=8 * height * width, transcendentals=0),
-    )(item_factors, region_factors, slab_blocks, block_rows, counts)
+    )(item_factors, region_factors, slab_blocks, jnp.transpose(block_rows, (2, 0, 1)), counts)
+    wide = region_factors.astype(f32)
+    return wide - region_rate * (region_grad + decay_rate * wide), new_items
 
 
 def solution(mesh):

time: 60.4 us -> 54.2 us (0.90)
  Pallas kernels: 54.4 us -> 49.4 us
  local copies, waits for them, and re-layouts: 5.13 us -> 0.66 us
  other arithmetic: 0 us -> 3.34 us
    pallas_call x1, Pallas kernels: 54.4 us -> 49.4 us  [on_device(): pl.pallas_call(functools.partial(kernel, R, Z, Y, chunk), out_shape=(jax....]
    unnamed x5, local copies, waits for them, and re-layouts: 5.13 us -> 0.66 us
    sub x0 -> x1, other arithmetic: none -> 3.34 us  [on_device(): return (wide - region_rate * (region_grad + decay_rate * wide), new_items)]
where the time goes in v2:
time: 54.2 us; the launch traced here: 54 us
  Pallas kernels  49.4 us (91%)
  other arithmetic  3.34 us (6%)
  local copies, waits for them, and re-layouts  0.66 us (1%)
  between operations  0.66 us (1%)
    pallas_call x1, Pallas kernels, on_device(): pl.pallas_call(functools.partial(kernel, R, Z, Y, chunk), out_shape=(jax....  49.4 us
    sub x1, other arithmetic, on_device(): return (wide - region_rate * (region_grad + decay_rate * wide), new_items)  3.34 us

profile of v2, /device:TPU:0, one launch (start us, length us, event | category | flops | bytes accessed | tf_op | source)
XLA Modules:
  0.0 54.0 jit_solution(3127420413033492940)
XLA Ops:
  0.6 0.0 copy-start
  0.6 49.4 %shard_map.68 = (f32[1024,512]{1,0:T(8,128)}, f32[1,64,512]{2,1,0:T(8,128)}) custom-call(bf16[1,64,512]{2,1,0:T(8,128)(2,1)} %items.1, bf16[1024,512]{1,0:T(8,128)(2,1)} %regions.1, bf16[1,16,6,128,128]{4,3,2,1,0:T(8,128)(2,1)} %slab.1, s32[6,1,16]{2,1,0:T(1,128)} %bitcast.1, s32[1,16]{1,0:T(1,128)} %counts.1), custom_call_target="tpu_custom_call" | custom-call | flops 6442450944 | bytes 4194304 | tf_op jit(solution)/shard_map/pallas_call | solution.py:292
  50.0 0.0 copy-done
  50.0 0.0 copy-start.1
  50.0 3.3 %convert_subtract_fusion = f32[1024,512]{1,0:T(8,128)} fusion(bf16[1024,512]{1,0:T(8,128)(2,1)S(1)} %copy-done, f32[1024,512]{1,0:T(8,128)} %get-tuple-element.4), kind=kLoop, calls=%fused_computation | loop fusion | flops 2621440 | bytes 5242880 | tf_op jit(solution)/shard_map/sub | solution.py:344
  53.4 0.0 copy-done.1
  53.4 0.7 %copy.8 = f32[1,64,512]{2,1,0:T(8,128)} copy(f32[1,64,512]{2,1,0:T(8,128)S(1)} %copy-done.1) | data formatting | bytes 262144
Async XLA Ops:
  0.6 49.4 %copy-start = (bf16[1024,512]{1,0:T(8,128)(2,1)S(1)}, bf16[1024,512]{1,0:T(8,128)(2,1)}, u32[]{:S(2)}) copy-start(bf16[1024,512]{1,0:T(8,128)(2,1)} %regions.1) | copy-start | bytes 3145732
  50.0 3.4 %copy-start.1 = (f32[1,64,512]{2,1,0:T(8,128)S(1)}, f32[1,64,512]{2,1,0:T(8,128)}, u32[]{:S(2)}) copy-start(f32[1,64,512]{2,1,0:T(8,128)} %get-tuple-element.9) | copy-start | bytes 393220

commit v3 on v2

--- a/solution.py
+++ b/solution.py
@@ -1,4 +1,5 @@
 import functools
+import math
 
 import jax
 import jax.numpy as jnp
@@ -238,31 +239,35 @@
     plane_next(1)
     share(0)
     plane_next(2)
+    forward(1)
     shared(0)
+    plane_next(3)
     load_u.wait()
     load_tiles.wait()
     for j in range(Z):
         last = j == Z - 1
         residuals(j)
         if not last:
-            forward(j + 1)
+            share(j + 1)
+        if j + 2 < Z:
+            forward(j + 2)
         if j > 0:
-            reduce_second(j - 1)
+            reduce_first(j - 1)
         gsend[j] = item_part(1 - k)
         send(gsend.at[j], grecv.at[j], gc, (j,), sibling)
-        if not last:
-            share(j + 1)
+        if j > 1:
+            reduce_third(j - 2)
         gown[j] = item_part(k)
-        plane_next(j + 3)
         if not last:
             region_part(j)
-        reduce_first(j)
-        if j > 0:
-            reduce_third(j - 1)
-        if not last:
+            if j > 0:
+                reduce_second(j - 1)
             shared(j + 1)
+    reduce_first(Z - 1)
+    reduce_second(Z - 2)
     region_part(Z - 1)
     reduce_second(Z - 1)
+    reduce_third(Z - 2)
     reduce_third(Z - 1)
     total = acc[...]
     for j in range(1, Z):
@@ -289,54 +294,58 @@
     chunk = 4 * block
     dma = pltpu.SemaphoreType.DMA
     vmem = pltpu.VMEM
+    buffers = [
+        vmem((height, width), bf16),
+        vmem((panels, slots, block, block), bf16),
+        vmem((Z, CORES * side, width), bf16),
+        vmem((height, CORES * side), bf16),
+        vmem((height, width), f32),
+        vmem((Z, side, width), f32),
+        vmem((Z, side, width), f32),
+        vmem((Z, side, width), f32),
+        vmem((Z, Y - 1, (R - 1) * n, half), bf16),
+        vmem((Z, Y - 1, (R - 1) * n, half), bf16),
+        vmem((Z, R - 1, (Y - 1) * n, half), bf16),
+        vmem((Z, R - 1, (Y - 1) * n, half), bf16),
+        vmem((Z, R - 1, n, width), bf16),
+        vmem((Z, R - 1, n, width), bf16),
+        vmem((Z, Y - 1, n, width), bf16),
+        vmem((Z, Y - 1, n, width), bf16),
+        vmem((Z - 1, n, width), bf16),
+        vmem((Z - 1, n, width), bf16),
+        vmem((n, width), f32),
+    ]
+    semaphores = [
+        dma((2,)),
+        dma((height // chunk,)),
+        dma((2, Z)),
+        dma((2, Z, R)),
+        dma((2, Z, Y)),
+        dma((2, Z, R, Y)),
+        dma((2, Z, R, Y)),
+        dma((2, Z)),
+        dma((2, Z)),
+        dma((2, Z, Y)),
+        dma((2, Z, R)),
+        dma((2, Z, R)),
+        dma((2, Z, Y)),
+        dma((2, Z)),
+    ]
+    held = sum(math.prod(buffer.shape) * jnp.dtype(buffer.dtype).itemsize for buffer in buffers)
     region_grad, new_items = pl.pallas_call(
         functools.partial(kernel, R, Z, Y, chunk),
         out_shape=(jax.ShapeDtypeStruct((height, width), f32), jax.ShapeDtypeStruct(item_factors.shape, f32)),
         in_specs=[
             pl.BlockSpec(memory_space=pltpu.VMEM),
-            pl.BlockSpec(memory_space=pl.ANY),
-            pl.BlockSpec(memory_space=pl.ANY),
+            pl.BlockSpec(memory_space=pltpu.HBM),
+            pl.BlockSpec(memory_space=pltpu.HBM),
             pl.BlockSpec(memory_space=pltpu.SMEM),
             pl.BlockSpec(memory_space=pltpu.SMEM),
         ],
         out_specs=(pl.BlockSpec(memory_space=pl.ANY), pl.BlockSpec(memory_space=pltpu.VMEM)),
-        scratch_shapes=[
-            vmem((height, width), bf16),
-            vmem((panels, slots, block, block), bf16),
-            vmem((Z, CORES * side, width), bf16),
-            vmem((height, CORES * side), bf16),
-            vmem((height, width), f32),
-            vmem((Z, side, width), f32),
-            vmem((Z, side, width), f32),
-            vmem((Z, side, width), f32),
-            vmem((Z, Y - 1, (R - 1) * n, half), bf16),
-            vmem((Z, Y - 1, (R - 1) * n, half), bf16),
-            vmem((Z, R - 1, (Y - 1) * n, half), bf16),
-            vmem((Z, R - 1, (Y - 1) * n, half), bf16),
-            vmem((Z, R - 1, n, width), bf16),
-            vmem((Z, R - 1, n, width), bf16),
-            vmem((Z, Y - 1, n, width), bf16),
-            vmem((Z, Y - 1, n, width), bf16),
-            vmem((Z - 1, n, width), bf16),
-            vmem((Z - 1, n, width), bf16),
-            vmem((n, width), f32),
-            dma((2,)),
-            dma((height // chunk,)),
-            dma((2, Z)),
-            dma((2, Z, R)),
-            dma((2, Z, Y)),
-            dma((2, Z, R, Y)),
-            dma((2, Z, R, Y)),
-            dma((2, Z)),
-            dma((2, Z)),
-            dma((2, Z, Y)),
-            dma((2, Z, R)),
-            dma((2, Z, R)),
-            dma((2, Z, Y)),
-            dma((2, Z)),
-        ],
+        scratch_shapes=buffers + semaphores,
         compiler_params=pltpu.CompilerParams(
-            collective_id=0, has_side_effects=True, vmem_limit_bytes=56 * 1024 * 1024),
+            collective_id=0, has_side_effects=True, vmem_limit_bytes=held + 8 * 1024 * 1024),
         cost_estimate=pl.CostEstimate(
             flops=6 * height * panels * block * width, bytes_accessed=8 * height * width, transcendentals=0),
     )(item_factors, region_factors, slab_blocks, jnp.transpose(block_rows, (2, 0, 1)), counts)

time: 54.2 us -> 54.6 us (level)
  local copies, waits for them, and re-layouts: 0.66 us -> 5.94 us
  Pallas kernels: 49.4 us -> 46.1 us
  other arithmetic: 3.34 us -> 1.69 us
    unnamed x5 -> x11, local copies, waits for them, and re-layouts: 0.66 us -> 5.94 us
    pallas_call x1, Pallas kernels: 49.4 us -> 46.1 us  [on_device(): pl.pallas_call(functools.partial(kernel, R, Z, Y, chunk), out_shape=(jax....]
    sub x1, other arithmetic: 3.34 us -> 1.69 us  [on_device(): return (wide - region_rate * (region_grad + decay_rate * wide), new_items)]
where the time goes in v3:
time: 54.6 us; the launch traced here: 54.4 us
  Pallas kernels  46.1 us (84%)
  local copies, waits for them, and re-layouts  5.94 us (11%)
  other arithmetic  1.69 us (3%)
  between operations  0.65 us (1%)
    pallas_call x1, Pallas kernels, on_device(): pl.pallas_call(functools.partial(kernel, R, Z, Y, chunk), out_shape=(jax....  46.1 us
    unnamed x11, local copies, waits for them, and re-layouts  5.94 us
    sub x1, other arithmetic, on_device(): return (wide - region_rate * (region_grad + decay_rate * wide), new_items)  1.69 us

profile of v3, /device:TPU:0, one launch (start us, length us, event | category | flops | bytes accessed | tf_op | source)
XLA Modules:
  0.0 54.4 jit_solution(10696464476201976764)
XLA Ops:
  0.6 0.0 copy-start
  0.6 1.2 %copy-done = bf16[1024,512]{1,0:T(8,128)(2,1)S(1)} copy-done((bf16[1024,512]{1,0:T(8,128)(2,1)S(1)}, bf16[1024,512]{1,0:T(8,128)(2,1)}, u32[]{:S(2)}) %copy-start) | copy-done | bytes 1048600
  1.9 0.0 copy-start.1
  1.9 1.9 %copy-done.1 = bf16[1,16,6,128,128]{4,3,2,1,0:T(8,128)(2,1)S(1)} copy-done((bf16[1,16,6,128,128]{4,3,2,1,0:T(8,128)(2,1)S(1)}, bf16[1,16,6,128,128]{4,3,2,1,0:T(8,128)(2,1)}, u32[]{:S(2)}) %copy-start.1) | copy-done | bytes 3145752
  3.7 0.0 copy-start.2
  3.7 0.8 %copy-done.2 = bf16[1,64,512]{2,1,0:T(8,128)(2,1)S(1)} copy-done((bf16[1,64,512]{2,1,0:T(8,128)(2,1)S(1)}, bf16[1,64,512]{2,1,0:T(8,128)(2,1)}, u32[]{:S(2)}) %copy-start.2) | copy-done | bytes 65560
  4.6 0.0 copy-start.3
  4.6 0.7 %copy-done.3 = s32[1,16,6]{1,0,2:T(1,128)S(1)} copy-done((s32[1,16,6]{1,0,2:T(1,128)S(1)}, s32[1,16,6]{1,0,2:T(1,128)}, u32[]{:S(2)}) %copy-start.3) | copy-done | bytes 408
  5.3 0.0 copy-start.4
  5.3 0.7 %copy-done.4 = s32[1,16]{1,0:T(1,128)S(1)} copy-done((s32[1,16]{1,0:T(1,128)S(1)}, s32[1,16]{1,0:T(1,128)}, u32[]{:S(2)}) %copy-start.4) | copy-done | bytes 88
  5.9 46.1 %shard_map.68 = (f32[1024,512]{1,0:T(8,128)S(1)}, f32[1,64,512]{2,1,0:T(8,128)S(1)}) custom-call(bf16[1,64,512]{2,1,0:T(8,128)(2,1)S(1)} %copy-done.2, bf16[1024,512]{1,0:T(8,128)(2,1)S(1)} %copy-done, bf16[1,16,6,128,128]{4,3,2,1,0:T(8,128)(2,1)S(1)} %copy-done.1, s32[6,1,16]{2,1,0:T(1,128)S(1)} %bitcast.1, s32[1,16]{1,0:T(1,128)S(1)} %copy-done.4), custom_call_target="tpu_custom_call" | custom-call | flops 6442450944 | bytes 4194304 | tf_op jit(solution)/shard_map/pallas_call | solution.py:335
  52.0 1.7 %convert_subtract_fusion = f32[1024,512]{1,0:T(8,128)} fusion(bf16[1024,512]{1,0:T(8,128)(2,1)S(1)} %copy-done, f32[1024,512]{1,0:T(8,128)S(1)} %get-tuple-element.4), kind=kLoop, calls=%fused_computation | loop fusion | flops 2621440 | bytes 5242880 | tf_op jit(solution)/shard_map/sub | solution.py:353
  53.7 0.7 %copy.8 = f32[1,64,512]{2,1,0:T(8,128)} copy(f32[1,64,512]{2,1,0:T(8,128)S(1)} %get-tuple-element.9) | data formatting | bytes 262144
Async XLA Ops:
  0.6 1.2 %copy-start = (bf16[1024,512]{1,0:T(8,128)(2,1)S(1)}, bf16[1024,512]{1,0:T(8,128)(2,1)}, u32[]{:S(2)}) copy-start(bf16[1024,512]{1,0:T(8,128)(2,1)} %regions.1) | copy-start | bytes 3145732
  1.9 1.9 %copy-start.1 = (bf16[1,16,6,128,128]{4,3,2,1,0:T(8,128)(2,1)S(1)}, bf16[1,16,6,128,128]{4,3,2,1,0:T(8,128)(2,1)}, u32[]{:S(2)}) copy-start(bf16[1,16,6,128,128]{4,3,2,1,0:T(8,128)(2,1)} %slab.1) | copy-start | bytes 9437188
  3.7 0.8 %copy-start.2 = (bf16[1,64,512]{2,1,0:T(8,128)(2,1)S(1)}, bf16[1,64,512]{2,1,0:T(8,128)(2,1)}, u32[]{:S(2)}) copy-start(bf16[1,64,512]{2,1,0:T(8,128)(2,1)} %items.1) | copy-start | bytes 196612
  4.6 0.7 %copy-start.3 = (s32[1,16,6]{1,0,2:T(1,128)S(1)}, s32[1,16,6]{1,0,2:T(1,128)}, u32[]{:S(2)}) copy-start(s32[1,16,6]{1,0,2:T(1,128)} %param.8) | copy-start | bytes 1156
  5.3 0.7 %copy-start.4 = (s32[1,16]{1,0:T(1,128)S(1)}, s32[1,16]{1,0:T(1,128)}, u32[]{:S(2)}) copy-start(s32[1,16]{1,0:T(1,128)} %counts.1) | copy-start | bytes 196

commit v4 on v3

--- a/solution.py
+++ b/solution.py
@@ -1,5 +1,4 @@
 import functools
-import math
 
 import jax
 import jax.numpy as jnp
@@ -15,7 +14,6 @@
 MESH = pl.DeviceIdType.MESH
 CORES = 2
 NT = (((1,), (1,)), ((), ()))
-TN = (((0,), (0,)), ((), ()))
 NN = (((1,), (0,)), ((), ()))
 
 
@@ -24,9 +22,9 @@
 
 
 def kernel(R, Z, Y, chunk, items, regions, slab, rows, counts, region_grad, new_items,
-           u, tiles, v, res, racc, gown, gsend, grecv,
+           u, tiles, v, res, ut, gkept, gown, gsend, grecv,
            s_a, r_a, s_b, r_b, s_x, r_x, s_y, r_y, s_z, r_z, acc,
-           loc_sem, out_sem, az, ax, ay, aa, ab, sib, gc, ga, gb, gx, gy, gz):
+           loc_sem, az, ax, ay, aa, ab, sib, gc, ga, gb, gx, gy, gz):
     x = lax.axis_index("row")
     c = lax.axis_index("col")
     k = lax.rem(c, CORES)
@@ -37,7 +35,6 @@
     half = width // 2
     n = block // R
     slots = tiles.shape[1]
-    chunks = u.shape[0] // chunk
 
     def col_of(zz, yy, kk):
         return (zz * Y + yy) * CORES + kk
@@ -155,7 +152,7 @@
                             (pred - tile) * live).astype(jnp.bfloat16)
             return carry
 
-        lax.fori_loop(0, chunks, body, 0)
+        lax.fori_loop(0, u.shape[0] // chunk, body, 0)
 
     def region_part(j):
         zz = zslot(j)
@@ -164,17 +161,15 @@
             here = pl.ds(pl.multiple_of(i * chunk, chunk), chunk)
             total = mm(res[here, :], v[zz], NN)
             if j > 0:
-                total = total + racc[here, :]
-            racc[here, :] = total
-            if j == Z - 1:
-                pltpu.make_async_copy(racc.at[here, :], region_grad.at[here, :], out_sem.at[i]).start()
+                total = total + region_grad[here, :]
+            region_grad[here, :] = total
             return carry
 
-        lax.fori_loop(0, chunks, body, 0)
+        lax.fori_loop(0, u.shape[0] // chunk, body, 0)
 
     def reduce_first(j):
         arrived(grecv.at[j], gc, (j,))
-        gown[j] = gown[j] + grecv[j]
+        gown[j] = jnp.transpose(gkept[j] + grecv[j])
         for dy in range(1, Y):
             yy = lax.rem(y + dy, Y)
             for dx in range(1, R):
@@ -223,7 +218,7 @@
             send(s_z.at[j - 1], r_z.at[j - 1], gz, (j,), zdev(j))
 
     def item_part(kk):
-        return mm(res[:, core_rows(kk)], u[...], TN)
+        return mm(ut[...], res[:, core_rows(kk)], NN)
 
     def plane_next(j):
         if j < Z:
@@ -237,12 +232,13 @@
         send(own, own, az, (d,), zdev(d))
     forward(0)
     plane_next(1)
+    load_u.wait()
+    ut[...] = jnp.transpose(u[...])
     share(0)
     plane_next(2)
     forward(1)
     shared(0)
     plane_next(3)
-    load_u.wait()
     load_tiles.wait()
     for j in range(Z):
         last = j == Z - 1
@@ -257,7 +253,7 @@
         send(gsend.at[j], grecv.at[j], gc, (j,), sibling)
         if j > 1:
             reduce_third(j - 2)
-        gown[j] = item_part(k)
+        gkept[j] = item_part(k)
         if not last:
             region_part(j)
             if j > 0:
@@ -278,20 +274,13 @@
     for copy in sent:
         copy.wait_send()
 
-    def finish(i, carry):
-        here = pl.ds(pl.multiple_of(i * chunk, chunk), chunk)
-        pltpu.make_async_copy(racc.at[here, :], region_grad.at[here, :], out_sem.at[i]).wait()
-        return carry
-
-    lax.fori_loop(0, chunks, finish, 0)
-
 
 def on_device(R, Z, Y, region_factors, item_factors, slab_blocks, block_rows, counts):
     bf16, f32 = jnp.bfloat16, jnp.float32
     height, width = region_factors.shape
     _, panels, slots, block, _ = slab_blocks.shape
     n, half, side = block // R, width // 2, Y * block
-    chunk = 4 * block
+    chunk = height
     dma = pltpu.SemaphoreType.DMA
     vmem = pltpu.VMEM
     buffers = [
@@ -299,10 +288,11 @@
         vmem((panels, slots, block, block), bf16),
         vmem((Z, CORES * side, width), bf16),
         vmem((height, CORES * side), bf16),
-        vmem((height, width), f32),
+        vmem((width, height), bf16),
+        vmem((Z, width, side), f32),
         vmem((Z, side, width), f32),
-        vmem((Z, side, width), f32),
-        vmem((Z, side, width), f32),
+        vmem((Z, width, side), f32),
+        vmem((Z, width, side), f32),
         vmem((Z, Y - 1, (R - 1) * n, half), bf16),
         vmem((Z, Y - 1, (R - 1) * n, half), bf16),
         vmem((Z, R - 1, (Y - 1) * n, half), bf16),
@@ -317,7 +307,6 @@
     ]
     semaphores = [
         dma((2,)),
-        dma((height // chunk,)),
         dma((2, Z)),
         dma((2, Z, R)),
         dma((2, Z, Y)),
@@ -331,10 +320,9 @@
         dma((2, Z, Y)),
         dma((2, Z)),
     ]
-    held = sum(math.prod(buffer.shape) * jnp.dtype(buffer.dtype).itemsize for buffer in buffers)
     region_grad, new_items = pl.pallas_call(
         functools.partial(kernel, R, Z, Y, chunk),
-        out_shape=(jax.ShapeDtypeStruct((height, width), f32), jax.ShapeDtypeStruct(item_factors.shape, f32)),
+        out_shape=(pltpu.VMEM((height, width), f32), pltpu.VMEM(item_factors.shape, f32)),
         in_specs=[
             pl.BlockSpec(memory_space=pltpu.VMEM),
             pl.BlockSpec(memory_space=pltpu.HBM),
@@ -342,10 +330,10 @@
             pl.BlockSpec(memory_space=pltpu.SMEM),
             pl.BlockSpec(memory_space=pltpu.SMEM),
         ],
-        out_specs=(pl.BlockSpec(memory_space=pl.ANY), pl.BlockSpec(memory_space=pltpu.VMEM)),
+        out_specs=(pl.BlockSpec(memory_space=pltpu.VMEM), pl.BlockSpec(memory_space=pltpu.VMEM)),
         scratch_shapes=buffers + semaphores,
         compiler_params=pltpu.CompilerParams(
-            collective_id=0, has_side_effects=True, vmem_limit_bytes=held + 8 * 1024 * 1024),
+            collective_id=0, has_side_effects=True, vmem_limit_bytes=56 * 1024 * 1024),
         cost_estimate=pl.CostEstimate(
             flops=6 * height * panels * block * width, bytes_accessed=8 * height * width, transcendentals=0),
     )(item_factors, region_factors, slab_blocks, jnp.transpose(block_rows, (2, 0, 1)), counts)

time: 54.6 us -> 49.4 us (0.905)
  local copies, waits for them, and re-layouts: 5.94 us -> 0.66 us
    unnamed x11 -> x3, local copies, waits for them, and re-layouts: 5.94 us -> 0.66 us
where the time goes in v4:
time: 49.4 us; the launch traced here: 49.3 us
  Pallas kernels  46.2 us (94%)
  other arithmetic  1.7 us (3%)
  local copies, waits for them, and re-layouts  0.66 us (1%)
  between operations  0.66 us (1%)
    pallas_call x1, Pallas kernels, on_device(): pl.pallas_call(functools.partial(kernel, R, Z, Y, chunk), out_shape=(pltp...  46.2 us
    sub x1, other arithmetic, on_device(): return (wide - region_rate * (region_grad + decay_rate * wide), new_items)  1.7 us

profile of v4, /device:TPU:0, one launch (start us, length us, event | category | flops | bytes accessed | tf_op | source)
XLA Modules:
  0.0 49.3 jit_solution(9138548750756991735)
XLA Ops:
  0.6 0.0 copy-start
  0.6 46.2 %shard_map.68 = (f32[1024,512]{1,0:T(8,128)S(1)}, f32[1,64,512]{2,1,0:T(8,128)S(1)}) custom-call(bf16[1,64,512]{2,1,0:T(8,128)(2,1)} %items.1, bf16[1024,512]{1,0:T(8,128)(2,1)} %regions.1, bf16[1,16,6,128,128]{4,3,2,1,0:T(8,128)(2,1)} %slab.1, s32[6,1,16]{2,1,0:T(1,128)} %bitcast.1, s32[1,16]{1,0:T(1,128)} %counts.1), custom_call_target="tpu_custom_call" | custom-call | flops 6442450944 | bytes 4194304 | tf_op jit(solution)/shard_map/pallas_call | solution.py:323
  46.9 0.0 copy-done
  46.9 1.7 %convert_subtract_fusion = f32[1024,512]{1,0:T(8,128)} fusion(bf16[1024,512]{1,0:T(8,128)(2,1)S(1)} %copy-done, f32[1024,512]{1,0:T(8,128)S(1)} %get-tuple-element.4), kind=kLoop, calls=%fused_computation | loop fusion | flops 2621440 | bytes 5242880 | tf_op jit(solution)/shard_map/sub | solution.py:341
  48.6 0.7 %copy.8 = f32[1,64,512]{2,1,0:T(8,128)} copy(f32[1,64,512]{2,1,0:T(8,128)S(1)} %get-tuple-element.7) | data formatting | bytes 262144
Async XLA Ops:
  0.6 46.3 %copy-start = (bf16[1024,512]{1,0:T(8,128)(2,1)S(1)}, bf16[1024,512]{1,0:T(8,128)(2,1)}, u32[]{:S(2)}) copy-start(bf16[1024,512]{1,0:T(8,128)(2,1)} %regions.1) | copy-start | bytes 3145732

commit v5 on v4

--- a/solution.py
+++ b/solution.py
@@ -169,7 +169,7 @@
 
     def reduce_first(j):
         arrived(grecv.at[j], gc, (j,))
-        gown[j] = jnp.transpose(gkept[j] + grecv[j])
+        gown[j] = jnp.transpose(gkept[j] + grecv[j].astype(jnp.float32))
         for dy in range(1, Y):
             yy = lax.rem(y + dy, Y)
             for dx in range(1, R):
@@ -249,7 +249,7 @@
             forward(j + 2)
         if j > 0:
             reduce_first(j - 1)
-        gsend[j] = item_part(1 - k)
+        gsend[j] = item_part(1 - k).astype(jnp.bfloat16)
         send(gsend.at[j], grecv.at[j], gc, (j,), sibling)
         if j > 1:
             reduce_third(j - 2)
@@ -291,8 +291,8 @@
         vmem((width, height), bf16),
         vmem((Z, width, side), f32),
         vmem((Z, side, width), f32),
-        vmem((Z, width, side), f32),
-        vmem((Z, width, side), f32),
+        vmem((Z, width, side), bf16),
+        vmem((Z, width, side), bf16),
         vmem((Z, Y - 1, (R - 1) * n, half), bf16),
         vmem((Z, Y - 1, (R - 1) * n, half), bf16),
         vmem((Z, R - 1, (Y - 1) * n, half), bf16),

time: 49.4 us -> 49.4 us (level)
  no operation moved by 1% of the time
where the time goes in v5:
time: 49.4 us; the launch traced here: 49.3 us
  Pallas kernels  46.3 us (94%)
  other arithmetic  1.7 us (3%)
  local copies, waits for them, and re-layouts  0.66 us (1%)
  between operations  0.66 us (1%)
    pallas_call x1, Pallas kernels, on_device(): pl.pallas_call(functools.partial(kernel, R, Z, Y, chunk), out_shape=(pltp...  46.3 us
    sub x1, other arithmetic, on_device(): return (wide - region_rate * (region_grad + decay_rate * wide), new_items)  1.7 us

profile of v5, /device:TPU:0, one launch (start us, length us, event | category | flops | bytes accessed | tf_op | source)
XLA Modules:
  0.0 49.3 jit_solution(16455230978309600510)
XLA Ops:
  0.6 0.0 copy-start
  0.6 46.3 %shard_map.68 = (f32[1024,512]{1,0:T(8,128)S(1)}, f32[1,64,512]{2,1,0:T(8,128)S(1)}) custom-call(bf16[1,64,512]{2,1,0:T(8,128)(2,1)} %items.1, bf16[1024,512]{1,0:T(8,128)(2,1)} %regions.1, bf16[1,16,6,128,128]{4,3,2,1,0:T(8,128)(2,1)} %slab.1, s32[6,1,16]{2,1,0:T(1,128)} %bitcast.1, s32[1,16]{1,0:T(1,128)} %counts.1), custom_call_target="tpu_custom_call" | custom-call | flops 6442450944 | bytes 4194304 | tf_op jit(solution)/shard_map/pallas_call | solution.py:323
  46.9 0.0 copy-done
  46.9 1.7 %convert_subtract_fusion = f32[1024,512]{1,0:T(8,128)} fusion(bf16[1024,512]{1,0:T(8,128)(2,1)S(1)} %copy-done, f32[1024,512]{1,0:T(8,128)S(1)} %get-tuple-element.4), kind=kLoop, calls=%fused_computation | loop fusion | flops 2621440 | bytes 5242880 | tf_op jit(solution)/shard_map/sub | solution.py:341
  48.6 0.7 %copy.8 = f32[1,64,512]{2,1,0:T(8,128)} copy(f32[1,64,512]{2,1,0:T(8,128)S(1)} %get-tuple-element.7) | data formatting | bytes 262144
Async XLA Ops:
  0.6 46.3 %copy-start = (bf16[1024,512]{1,0:T(8,128)(2,1)S(1)}, bf16[1024,512]{1,0:T(8,128)(2,1)}, u32[]{:S(2)}) copy-start(bf16[1024,512]{1,0:T(8,128)(2,1)} %regions.1) | copy-start | bytes 3145732

commit v6 on v4

--- a/solution.py
+++ b/solution.py
@@ -24,7 +24,7 @@
 def kernel(R, Z, Y, chunk, items, regions, slab, rows, counts, region_grad, new_items,
            u, tiles, v, res, ut, gkept, gown, gsend, grecv,
            s_a, r_a, s_b, r_b, s_x, r_x, s_y, r_y, s_z, r_z, acc,
-           loc_sem, az, ax, ay, aa, ab, sib, gc, ga, gb, gx, gy, gz):
+           places, loc_sem, az, ax, ay, aa, ab, sib, gc, ga, gb, gx, gy, gz):
     x = lax.axis_index("row")
     c = lax.axis_index("col")
     k = lax.rem(c, CORES)
@@ -128,6 +128,19 @@
     def shared(j):
         arrived(v.at[zslot(j), core_rows(1 - k)], sib, (j,))
 
+    def find_places():
+        def body(p, carry):
+            count = counts[0, p]
+            listed = [jnp.where(count > s, rows[s, 0, p], -1) for s in range(slots)]
+            for b in range(places.shape[1]):
+                found = jnp.int32(0)
+                for s in range(slots):
+                    found = jnp.where(listed[s] == b, s + 1, found)
+                places[p, b] = found
+            return carry
+
+        lax.fori_loop(0, places.shape[0], body, 0)
+
     def residuals(j):
         zz = zslot(j)
 
@@ -138,13 +151,9 @@
                 for yy in range(Y):
                     left = (kk * Y + yy) * block
                     p = col_of(zz, yy, kk)
-                    count = counts[0, p]
                     for part in range(chunk // block):
                         b = i * (chunk // block) + part
-                        found = jnp.int32(0)
-                        for s in range(slots):
-                            hit = (rows[s, 0, p] == b) & (count > s)
-                            found = jnp.where(hit, s + 1, found)
+                        found = places[p, b]
                         live = jnp.where(found > 0, jnp.float32(1), jnp.float32(0))
                         tile = tiles[p, jnp.maximum(found - 1, 0)].astype(jnp.float32)
                         pred = predicted[part * block:(part + 1) * block, left:left + block]
@@ -230,6 +239,7 @@
     plane_start(0)
     for d in range(1, Z):
         send(own, own, az, (d,), zdev(d))
+    find_places()
     forward(0)
     plane_next(1)
     load_u.wait()
@@ -305,7 +315,8 @@
         vmem((Z - 1, n, width), bf16),
         vmem((n, width), f32),
     ]
-    semaphores = [
+    small = [
+        pltpu.SMEM((panels, height // block), jnp.int32),
         dma((2,)),
         dma((2, Z)),
         dma((2, Z, R)),
@@ -331,7 +342,7 @@
             pl.BlockSpec(memory_space=pltpu.SMEM),
         ],
         out_specs=(pl.BlockSpec(memory_space=pltpu.VMEM), pl.BlockSpec(memory_space=pltpu.VMEM)),
-        scratch_shapes=buffers + semaphores,
+        scratch_shapes=buffers + small,
         compiler_params=pltpu.CompilerParams(
             collective_id=0, has_side_effects=True, vmem_limit_bytes=56 * 1024 * 1024),
         cost_estimate=pl.CostEstimate(

time: 49.4 us -> 49.4 us (level)
  no operation moved by 1% of the time
where the time goes in v6:
time: 49.4 us; the launch traced here: 49.3 us
  Pallas kernels  46.2 us (94%)
  other arithmetic  1.7 us (3%)
  local copies, waits for them, and re-layouts  0.66 us (1%)
  between operations  0.66 us (1%)
    pallas_call x1, Pallas kernels, on_device(): pl.pallas_call(functools.partial(kernel, R, Z, Y, chunk), out_shape=(pltp...  46.2 us
    sub x1, other arithmetic, on_device(): return (wide - region_rate * (region_grad + decay_rate * wide), new_items)  1.7 us

profile of v6, /device:TPU:0, one launch (start us, length us, event | category | flops | bytes accessed | tf_op | source)
XLA Modules:
  0.0 49.3 jit_solution(12686575361207628882)
XLA Ops:
  0.6 0.0 copy-start
  0.6 46.2 %shard_map.68 = (f32[1024,512]{1,0:T(8,128)S(1)}, f32[1,64,512]{2,1,0:T(8,128)S(1)}) custom-call(bf16[1,64,512]{2,1,0:T(8,128)(2,1)} %items.1, bf16[1024,512]{1,0:T(8,128)(2,1)} %regions.1, bf16[1,16,6,128,128]{4,3,2,1,0:T(8,128)(2,1)} %slab.1, s32[6,1,16]{2,1,0:T(1,128)} %bitcast.1, s32[1,16]{1,0:T(1,128)} %counts.1), custom_call_target="tpu_custom_call" | custom-call | flops 6442450944 | bytes 4194304 | tf_op jit(solution)/shard_map/pallas_call | solution.py:334
  46.9 0.0 copy-done
  46.9 1.7 %convert_subtract_fusion = f32[1024,512]{1,0:T(8,128)} fusion(bf16[1024,512]{1,0:T(8,128)(2,1)S(1)} %copy-done, f32[1024,512]{1,0:T(8,128)S(1)} %get-tuple-element.4), kind=kLoop, calls=%fused_computation | loop fusion | flops 2621440 | bytes 5242880 | tf_op jit(solution)/shard_map/sub | solution.py:352
  48.6 0.7 %copy.8 = f32[1,64,512]{2,1,0:T(8,128)} copy(f32[1,64,512]{2,1,0:T(8,128)S(1)} %get-tuple-element.7) | data formatting | bytes 262144
Async XLA Ops:
  0.6 46.3 %copy-start = (bf16[1024,512]{1,0:T(8,128)(2,1)S(1)}, bf16[1024,512]{1,0:T(8,128)(2,1)}, u32[]{:S(2)}) copy-start(bf16[1024,512]{1,0:T(8,128)(2,1)} %regions.1) | copy-start | bytes 3145732

commit v7 on v6

--- a/solution.py
+++ b/solution.py
@@ -253,27 +253,24 @@
     for j in range(Z):
         last = j == Z - 1
         residuals(j)
+        gsend[j] = item_part(1 - k)
+        send(gsend.at[j], grecv.at[j], gc, (j,), sibling)
+        gkept[j] = item_part(k)
+        if j > 0:
+            reduce_second(j - 1)
+        if last:
+            reduce_first(j)
+        region_part(j)
         if not last:
+            reduce_first(j)
             share(j + 1)
         if j + 2 < Z:
             forward(j + 2)
         if j > 0:
-            reduce_first(j - 1)
-        gsend[j] = item_part(1 - k)
-        send(gsend.at[j], grecv.at[j], gc, (j,), sibling)
-        if j > 1:
-            reduce_third(j - 2)
-        gkept[j] = item_part(k)
+            reduce_third(j - 1)
         if not last:
-            region_part(j)
-            if j > 0:
-                reduce_second(j - 1)
             shared(j + 1)
-    reduce_first(Z - 1)
-    reduce_second(Z - 2)
-    region_part(Z - 1)
     reduce_second(Z - 1)
-    reduce_third(Z - 2)
     reduce_third(Z - 1)
     total = acc[...]
     for j in range(1, Z):

time: 49.4 us -> 50.3 us (1.018)
  Pallas kernels: 46.2 us -> 47.1 us
    pallas_call x1, Pallas kernels: 46.2 us -> 47.1 us  [on_device(): pl.pallas_call(functools.partial(kernel, R, Z, Y, chunk), out_shape=(pltp...]
where the time goes in v7:
time: 50.3 us; the launch traced here: 50.1 us
  Pallas kernels  47.1 us (94%)
  other arithmetic  1.7 us (3%)
  local copies, waits for them, and re-layouts  0.66 us (1%)
  between operations  0.66 us (1%)
    pallas_call x1, Pallas kernels, on_device(): pl.pallas_call(functools.partial(kernel, R, Z, Y, chunk), out_shape=(pltp...  47.1 us
    sub x1, other arithmetic, on_device(): return (wide - region_rate * (region_grad + decay_rate * wide), new_items)  1.7 us

profile of v7, /device:TPU:0, one launch (start us, length us, event | category | flops | bytes accessed | tf_op | source)
XLA Modules:
  0.0 50.1 jit_solution(15787750323826501569)
XLA Ops:
  0.6 0.0 copy-start
  0.6 47.1 %shard_map.68 = (f32[1024,512]{1,0:T(8,128)S(1)}, f32[1,64,512]{2,1,0:T(8,128)S(1)}) custom-call(bf16[1,64,512]{2,1,0:T(8,128)(2,1)} %items.1, bf16[1024,512]{1,0:T(8,128)(2,1)} %regions.1, bf16[1,16,6,128,128]{4,3,2,1,0:T(8,128)(2,1)} %slab.1, s32[6,1,16]{2,1,0:T(1,128)} %bitcast.1, s32[1,16]{1,0:T(1,128)} %counts.1), custom_call_target="tpu_custom_call" | custom-call | flops 6442450944 | bytes 4194304 | tf_op jit(solution)/shard_map/pallas_call | solution.py:331
  47.8 0.0 copy-done
  47.8 1.7 %convert_subtract_fusion = f32[1024,512]{1,0:T(8,128)} fusion(bf16[1024,512]{1,0:T(8,128)(2,1)S(1)} %copy-done, f32[1024,512]{1,0:T(8,128)S(1)} %get-tuple-element.4), kind=kLoop, calls=%fused_computation | loop fusion | flops 2621440 | bytes 5242880 | tf_op jit(solution)/shard_map/sub | solution.py:349
  49.5 0.7 %copy.8 = f32[1,64,512]{2,1,0:T(8,128)} copy(f32[1,64,512]{2,1,0:T(8,128)S(1)} %get-tuple-element.7) | data formatting | bytes 262144
Async XLA Ops:
  0.6 47.1 %copy-start = (bf16[1024,512]{1,0:T(8,128)(2,1)S(1)}, bf16[1024,512]{1,0:T(8,128)(2,1)}, u32[]{:S(2)}) copy-start(bf16[1024,512]{1,0:T(8,128)(2,1)} %regions.1) | copy-start | bytes 3145732
